TPU v7x, 128 devices: a whole 4x4x4 slice. The times are simulated.
128 devices in a mesh: tm: 16 (over y_lo, z, core), rows: 8 (over y_hi, x).
Axes of the slice: x: 4, y: 4 (y_hi: 2, y_lo: 2; y = y_hi * 2 + y_lo), z: 4, core: 2. Of those that a mesh axis runs over, the one named last changes fastest.
Arguments:
- activations: bfloat16 [128, 32, 32, 384], P('tm', 'rows'), may hold values from -27 to 27
- frame_counts: int32 [16], replicated, may hold values from 1 to 8, as said below
- norm_gain: float32 [384], replicated, may hold values from 0.5 to 1.5
- norm_bias: float32 [384], replicated, may hold values from -3 to 3
- conv_weight: bfloat16 [10368, 384], replicated, may hold values from -0.0625 to 0.0625
- cotangent: bfloat16 [128, 32, 32, 384], P('tm', 'rows'), may hold values from -6 to 6
Outputs:
- block_out: bfloat16 [128, 32, 32, 384], P('tm', 'rows')
- input_grad: float32 [128, 32, 32, 384], P('tm', 'rows')
- weight_grad: float32 [10368, 384], P(('tm', 'rows'))
Inputs may be any that keep to these rules, and one draw needn't show every extreme that they name: `frame_counts`: entry 0 is 1; every other entry is 4 or 8, and 8 occurs; the entries sum to 89.
All inputs are finite; a program needn't handle non-finite values.
Results may differ from a plain program's by a relative error of at most 0.0028.
Values may be sent and summed in bfloat16 or wider, within the bound.
No kernel may reach another device: no remote copies, remote signals or barrier semaphores. Data moves between devices by JAX's collectives and lax.ppermute only.
A program may use at most 256 MiB of HBM per device.

v0:
```python
import math

import jax
import jax.numpy as jnp
import numpy as np
from jax import lax
from jax.experimental import pallas as pl
from jax.experimental.pallas import tpu as pltpu
from jax.sharding import Mesh
from jax.sharding import PartitionSpec as P

GROUPS = 32
EPS = 1e-05
CHAN = 384
HALF = CHAN // 2
SLOTS = 8
ROWS = 4
COLS = 32
CELLS = ROWS * COLS
POS = SLOTS * CELLS
WIDE = 3 * CHAN
PIECE = 81
CHIPS = 64
LANES = 128
WIDE_CELLS = (ROWS + 2) * COLS
CELL_COUNT = 8 * CELLS * (CHAN // GROUPS)
TILE = 256

TM = ("ylo", "z", "core")
ROW_AXES = ("yhi", "x")
CHIP_AXES = ("ylo", "z", "yhi", "x")
ALL_AXES = TM + ROW_AXES

bf16 = jnp.bfloat16
f32 = jnp.float32
VMEM_LIMIT = pltpu.CompilerParams(vmem_limit_bytes=64 * 1024 * 1024)


def from_left(values):
    col = lax.broadcasted_iota(jnp.int32, values.shape, 0) % COLS
    return jnp.where(col == 0, 0.0, pltpu.roll(values, 1, 0))


def from_right(values):
    col = lax.broadcasted_iota(jnp.int32, values.shape, 0) % COLS
    return jnp.where(col == COLS - 1, 0.0, pltpu.roll(values, values.shape[0] - 1, 0))


def tap_products(x_ref, w_ref, acc, back):
    step = pl.program_id(0)
    weights = w_ref[...]
    pieces = []
    for b in range(3):
        at = (2 - step, 2 - b) if back else (step, b)
        pieces.append(x_ref[pl.ds(at[0], SLOTS), pl.ds(at[1], ROWS)].reshape(POS, CHAN))
    left = jnp.concatenate(pieces, axis=1)
    if back:
        right = jnp.concatenate([weights[b * WIDE : (b + 1) * WIDE] for b in range(3)], axis=1)
        dims = (((1,), (1,)), ((), ()))
    else:
        right = jnp.concatenate(
            [
                jnp.concatenate(
                    [weights[(b * 3 + c) * CHAN : (b * 3 + c + 1) * CHAN] for c in range(3)], axis=1
                )
                for b in range(3)
            ],
            axis=0,
        )
        dims = (((1,), (0,)), ((), ()))
    product = lax.dot_general(left, right, dims, preferred_element_type=f32)

    @pl.when(step == 0)
    def _():
        acc[...] = product

    @pl.when(step > 0)
    def _():
        acc[...] += product


def forward_kernel(place_ref, before_ref, hidden_ref, w_ref, act_ref, out_ref, x, acc):
    @pl.when(pl.program_id(0) == 0)
    def _():
        x[:2] = before_ref[...]
        x[2:] = hidden_ref[...]

    tap_products(x, w_ref, acc, False)

    @pl.when(pl.program_id(0) == 2)
    def _():
        for frame in range(SLOTS):
            rows = slice(frame * CELLS, (frame + 1) * CELLS)
            conv = (
                acc[rows, CHAN : 2 * CHAN]
                + from_left(acc[rows, :CHAN])
                + from_right(acc[rows, 2 * CHAN :])
            )
            total = act_ref[rows].astype(f32) + conv
            out_ref[rows] = jnp.where(frame < place_ref[0], total, 0.0).astype(bf16)


def backward_kernel(
    place_ref,
    cot_ref,
    low_ref,
    high_ref,
    head_ref,
    w_ref,
    act_ref,
    mean_ref,
    inv_ref,
    gain_ref,
    bias_ref,
    out_ref,
    first_ref,
    second_ref,
    x,
    acc,
):
    @pl.when(pl.program_id(0) == 0)
    def _():
        count = place_ref[0]
        for frame in range(SLOTS):

            @pl.when(frame < count)
            def _(frame=frame):
                x[frame, 0] = low_ref[SLOTS + frame, 0]
                x[frame, 1 : 1 + ROWS] = cot_ref[frame]
                x[frame, 1 + ROWS] = high_ref[SLOTS + frame, 0]

            @pl.when(frame >= count)
            def _(frame=frame):
                x[frame] = jnp.zeros((ROWS + 2, COLS, CHAN), bf16)

        x[SLOTS:] = jnp.zeros((2, ROWS + 2, COLS, CHAN), bf16)
        x[pl.ds(count, 2)] = head_ref[...]

    tap_products(x, w_ref, acc, True)

    @pl.when(pl.program_id(0) == 2)
    def _():
        gain = gain_ref[...]
        bias = bias_ref[...]
        for frame in range(SLOTS):
            rows = slice(frame * CELLS, (frame + 1) * CELLS)
            grad = (
                acc[rows, CHAN : 2 * CHAN]
                + from_right(acc[rows, :CHAN])
                + from_left(acc[rows, 2 * CHAN :])
            )
            centred = (act_ref[rows].astype(f32) - mean_ref[frame : frame + 1]) * inv_ref[
                frame : frame + 1
            ]
            pre_act = centred * gain + bias
            gate = jax.nn.sigmoid(pre_act)
            pre_grad = grad * gate * (1.0 + pre_act * (1.0 - gate)) * gain
            out_ref[rows] = pre_grad
            first_ref[frame : frame + 1] = jnp.sum(pre_grad, axis=0, keepdims=True)
            second_ref[frame : frame + 1] = jnp.sum(pre_grad * centred, axis=0, keepdims=True)


READY = ((0, 2), (2, 5), (5, 8))


def weight_kernel(
    place_ref,
    hidden_ref,
    other_ref,
    even_ref,
    odd_ref,
    cot_ref,
    other_cot_ref,
    out_ref,
    before_ref,
    other_before,
    turned,
    right,
    sums,
    packed,
    sems,
):
    core = place_ref[1]

    def last_two(ref, count, to_ref):
        @pl.when(count >= 2)
        def _():
            to_ref[...] = ref[pl.ds(jnp.maximum(count - 2, 0), 2)]

        @pl.when(count < 2)
        def _():
            to_ref[0] = jnp.zeros((ROWS + 2, COLS, CHAN), bf16)
            to_ref[1] = ref[0]

    @pl.when(core == 0)
    def _():
        before_ref[...] = even_ref[...]
        last_two(hidden_ref, place_ref[0], other_before)

    @pl.when(core == 1)
    def _():
        other_before[...] = odd_ref[...]
        last_two(other_ref, place_ref[3], before_ref)

    def turn(ref, f, column):
        for b in range(3):
            values = ref[f, b : b + ROWS].reshape(CELLS, CHAN)
            turned[b * CHAN : (b + 1) * CHAN, pl.ds(pl.multiple_of(column, CELLS), CELLS)] = values.T

    for block, (early, late) in enumerate(((before_ref, hidden_ref), (other_before, other_ref))):
        base = block * (SLOTS + 2) * CELLS
        for f in range(2):
            turn(early, f, base + f * CELLS)

        def turn_late(f, carry, late=late, base=base):
            turn(late, f, base + (f + 2) * CELLS)
            return carry

        lax.fori_loop(0, SLOTS, turn_late, 0, unroll=True)

    left_lanes = lax.broadcasted_iota(jnp.int32, (CELLS, LANES), 1) < LANES // 2

    def move(f, carry):
        for block, ref in enumerate((cot_ref, other_cot_ref)):
            values = ref[f].reshape(CELLS, CHAN).astype(f32)
            values = jnp.where(f < place_ref[3 * block], values, 0.0)
            middle = values[:, LANES : 2 * LANES]
            swapped = pltpu.roll(middle, LANES // 2, 1)
            first = core == 0
            outer = jnp.where(first, values[:, :LANES], values[:, 2 * LANES :])
            inner = jnp.where(left_lanes == first, middle, swapped)
            chosen = jnp.concatenate([outer, inner], axis=1)
            rows = pl.ds(pl.multiple_of(block * POS + f * CELLS, CELLS), CELLS)
            for c, moved in enumerate((from_right(chosen), chosen, from_left(chosen))):
                right[rows, c * TILE : (c + 1) * TILE] = moved.astype(bf16)
        return carry

    lax.fori_loop(0, SLOTS, move, 0, unroll=True)

    upper = lax.broadcasted_iota(jnp.int32, (PIECE, LANES), 1) >= LANES // 2
    copies = []
    for a in range(3):
        window = jnp.concatenate(
            [
                turned[:, start : start + POS]
                for block in range(2)
                for start in [(block * (SLOTS + 2) + a) * CELLS]
            ],
            axis=1,
        )
        product = jnp.dot(window, right[...], preferred_element_type=f32)
        for b in range(3):
            for c in range(3):
                at = ((a * 3 + b) * 3 + c) * CHAN
                sums[at : at + CHAN] = product[
                    b * CHAN : (b + 1) * CHAN, c * TILE : (c + 1) * TILE
                ]
        for chip in range(8 * READY[a][0], 8 * READY[a][1]):
            start = 1296 * (chip // 8) + PIECE * (chip % 8)
            first, second = sums[start : start + PIECE], sums[start + 648 : start + 648 + PIECE]
            block = jnp.concatenate(
                [
                    first[:, :LANES],
                    second[:, :LANES],
                    jnp.where(upper, second[:, LANES:], first[:, LANES:]),
                ],
                axis=0,
            )
            packed[chip] = block.astype(bf16)
        chips = pl.ds(8 * READY[a][0], 8 * (READY[a][1] - READY[a][0]))
        copies.append(pltpu.make_async_copy(packed.at[chips], out_ref.at[chips], sems.at[a]))
        copies[-1].start()
    for copy in copies:
        copy.wait()


def sums_kernel(act_ref, out_ref):
    firsts, seconds = [], []
    for frame in range(SLOTS):
        values = act_ref[frame].reshape(CELLS, CHAN).astype(f32)
        firsts.append(jnp.sum(values, axis=0, keepdims=True))
        seconds.append(jnp.sum(values * values, axis=0, keepdims=True))
    both = jnp.concatenate(firsts + seconds, axis=0)
    for peer in range(8):
        out_ref[peer] = both


def group_means(sums, same_ref):
    return jnp.dot(
        sums, same_ref[...], precision=lax.Precision.HIGHEST, preferred_element_type=f32
    ) * (1.0 / CELL_COUNT)


def hidden_kernel(
    place_ref,
    peers_ref,
    same_ref,
    act_ref,
    low_ref,
    high_ref,
    cot_ref,
    cot_low_ref,
    cot_high_ref,
    gain_ref,
    bias_ref,
    hidden_ref,
    pair_ref,
    head_ref,
    mean_ref,
    inv_ref,
):
    step = pl.program_id(0)
    count, row_place = place_ref[0], place_ref[2]

    @pl.when(step == 0)
    def _():
        total = peers_ref[0]
        for peer in range(1, 8):
            total = total + peers_ref[peer]
        stats = group_means(total, same_ref)
        mean_ref[...] = stats[:SLOTS]
        inv_ref[...] = lax.rsqrt(stats[SLOTS:] - stats[:SLOTS] * stats[:SLOTS] + EPS)
        pair_ref[0] = jnp.zeros((ROWS + 2, COLS, CHAN), bf16)
        head_ref[:, :1] = cot_low_ref[...]
        head_ref[:, 1 : 1 + ROWS] = cot_ref[...]
        head_ref[:, 1 + ROWS :] = cot_high_ref[...]

    gain = gain_ref[...]
    bias = bias_ref[...]
    for k in range(4):
        frame = step * 4 + k
        live = frame < count
        mean = mean_ref[pl.ds(frame, 1)]
        inv = inv_ref[pl.ds(frame, 1)]

        def activated(values, keep, mean=mean, inv=inv):
            pre_act = (values.astype(f32) - mean) * inv * gain + bias
            return jnp.where(keep, pre_act * jax.nn.sigmoid(pre_act), 0.0).astype(bf16)

        hidden = activated(act_ref[k].reshape(CELLS, CHAN), live)
        hidden_ref[k, 1 : 1 + ROWS] = hidden.reshape(ROWS, COLS, CHAN)
        hidden_ref[k, 0] = activated(low_ref[k, 0], live & (row_place > 0))
        hidden_ref[k, 1 + ROWS] = activated(high_ref[k, 0], live & (row_place < 7))
        for late in range(2):

            @pl.when(frame == count - 2 + late)
            def _(k=k, late=late):
                pair_ref[late] = hidden_ref[k]


def whole(shape):
    return pl.BlockSpec(shape, lambda step: (0,) * len(shape))


def cost(flops, moved):
    return pl.CostEstimate(flops=flops, bytes_accessed=moved, transcendentals=0)


FLOPS = 2 * POS * 27 * CHAN * CHAN
TAPS_SPEC = pl.BlockSpec((3 * WIDE, CHAN), lambda step: (step, 0))


def forward_conv(place, before, hidden, weights, act):
    return pl.pallas_call(
        forward_kernel,
        out_shape=jax.ShapeDtypeStruct((POS, CHAN), bf16),
        grid=(3,),
        in_specs=[
            SMEM_SPEC,
            whole(before.shape),
            whole(hidden.shape),
            TAPS_SPEC,
            whole(act.shape),
        ],
        out_specs=whole((POS, CHAN)),
        scratch_shapes=[
            pltpu.VMEM((SLOTS + 2, ROWS + 2, COLS, CHAN), bf16),
            pltpu.VMEM((POS, WIDE), f32),
        ],
        compiler_params=VMEM_LIMIT,
        cost_estimate=cost(FLOPS, 12 << 20),
        name="forward_conv",
    )(place, before, hidden, weights, act)


def backward_conv(place, cot, low, high, head, weights, act, mean, inv, gain, bias):
    smalls = [mean, inv, gain, bias]
    return pl.pallas_call(
        backward_kernel,
        out_shape=(
            jax.ShapeDtypeStruct((POS, CHAN), f32),
            jax.ShapeDtypeStruct((SLOTS, CHAN), f32),
            jax.ShapeDtypeStruct((SLOTS, CHAN), f32),
        ),
        grid=(3,),
        in_specs=[SMEM_SPEC]
        + [whole(v.shape) for v in (cot, low, high, head)]
        + [TAPS_SPEC, whole(act.shape)]
        + [whole(v.shape) for v in smalls],
        out_specs=(whole((POS, CHAN)), whole((SLOTS, CHAN)), whole((SLOTS, CHAN))),
        scratch_shapes=[
            pltpu.VMEM((SLOTS + 2, ROWS + 2, COLS, CHAN), bf16),
            pltpu.VMEM((POS, WIDE), f32),
        ],
        compiler_params=VMEM_LIMIT,
        cost_estimate=cost(FLOPS, 12 << 20),
        name="backward_conv",
    )(place, cot, low, high, head, weights, act, *smalls)


def local_sums(act):
    return pl.pallas_call(
        sums_kernel,
        out_shape=jax.ShapeDtypeStruct((8, 2 * SLOTS, CHAN), f32),
        compiler_params=VMEM_LIMIT,
        cost_estimate=cost(4 * POS * CHAN, 1 << 20),
        name="local_sums",
    )(act)


SMEM_SPEC = pl.BlockSpec(memory_space=pltpu.SMEM)


def same_group():
    group = np.arange(CHAN) // (CHAN // GROUPS)
    return jnp.asarray((group[:, None] == group[None, :]).astype(np.float32))


def frames_spec(*rest, first=0, count=4, last=1):
    return pl.BlockSpec(
        (count,) + rest,
        lambda step: (first // count + jnp.minimum(step, last),) + (0,) * len(rest),
    )


def make_hidden(place, peers, act, cot, low, high, gain, bias):
    wide = (ROWS + 2, COLS, CHAN)
    return pl.pallas_call(
        hidden_kernel,
        out_shape=(
            jax.ShapeDtypeStruct((SLOTS,) + wide, bf16),
            jax.ShapeDtypeStruct((2,) + wide, bf16),
            jax.ShapeDtypeStruct((2,) + wide, bf16),
            jax.ShapeDtypeStruct((SLOTS, CHAN), f32),
            jax.ShapeDtypeStruct((SLOTS, CHAN), f32),
        ),
        grid=(2,),
        in_specs=[
            SMEM_SPEC,
            whole(peers.shape),
            whole((CHAN, CHAN)),
            frames_spec(ROWS, COLS, CHAN),
            frames_spec(1, COLS, CHAN),
            frames_spec(1, COLS, CHAN),
            frames_spec(ROWS, COLS, CHAN, count=2, last=0),
            frames_spec(1, COLS, CHAN, first=SLOTS, count=2, last=0),
            frames_spec(1, COLS, CHAN, first=SLOTS, count=2, last=0),
            whole((1, CHAN)),
            whole((1, CHAN)),
        ],
        out_specs=(
            frames_spec(*wide),
            whole((2,) + wide),
            whole((2,) + wide),
            whole((SLOTS, CHAN)),
            whole((SLOTS, CHAN)),
        ),
        compiler_params=VMEM_LIMIT,
        cost_estimate=cost(40 * POS * CHAN, 5 << 20),
        name="make_hidden",
    )(place, peers, same_group(), act, low, high, cot, low, high, gain, bias)


def weight_terms(place, hidden, other, even, odd, cot, other_cot):
    in_vmem = pl.BlockSpec(memory_space=pltpu.VMEM)
    pair = (2, ROWS + 2, COLS, CHAN)
    return pl.pallas_call(
        weight_kernel,
        out_shape=(
            jax.ShapeDtypeStruct((CHIPS, 3 * PIECE, LANES), bf16),
            jax.ShapeDtypeStruct(pair, bf16),
        ),
        in_specs=[SMEM_SPEC] + [in_vmem] * 6,
        out_specs=(pl.BlockSpec(memory_space=pl.ANY), in_vmem),
        scratch_shapes=[
            pltpu.VMEM(pair, bf16),
            pltpu.VMEM((WIDE, 2 * (SLOTS + 2) * CELLS), bf16),
            pltpu.VMEM((2 * POS, 3 * TILE), bf16),
            pltpu.VMEM((9 * WIDE, TILE), f32),
            pltpu.VMEM((CHIPS, 3 * PIECE, LANES), bf16),
            pltpu.SemaphoreType.DMA((3,)),
        ],
        compiler_params=VMEM_LIMIT,
        cost_estimate=cost(FLOPS, 12 << 20),
        name="weight_terms",
    )(place, hidden, other, even, odd, cot, other_cot)


def shift(values, axes, count, step):
    pairs = [(i, i + step) for i in range(count) if 0 <= i + step < count]
    return lax.ppermute(values, axes, pairs)


def swap_cores(values):
    return lax.ppermute(values, "core", [(0, 1), (1, 0)])


def edge_rows(block):
    low = shift(block[:, ROWS - 1 :], ROW_AXES, 8, 1)
    high = shift(block[:, :1], ROW_AXES, 8, -1)
    return low, high


def per_group(first, second):
    grouped = jnp.concatenate([first, second], axis=0).reshape(2 * SLOTS, GROUPS, CHAN // GROUPS)
    return jnp.sum(grouped, axis=2)


def per_channel(grouped):
    return jnp.repeat(grouped, CHAN // GROUPS, axis=1)


def on_device(activations, frame_counts, norm_gain, norm_bias, conv_weight, cotangent):
    core = lax.axis_index("core")
    act = activations.reshape(POS, CHAN)
    gain, bias = norm_gain[None], norm_bias[None]

    sums = local_sums(activations)
    peers = lax.all_to_all(sums, ROW_AXES, 0, 0)
    source, rows_at_once, _ = lax.optimization_barrier((activations, cotangent, sums))
    low, high = edge_rows(jnp.concatenate([source, rows_at_once], 0))
    other_cot = swap_cores(rows_at_once)
    low, high, peers, other_cot = lax.optimization_barrier((low, high, peers, other_cot))

    tm = lax.axis_index(TM)
    count = frame_counts[tm]
    place = jnp.stack(
        [count, core, lax.axis_index(ROW_AXES), frame_counts[tm + 1 - 2 * core]]
    )
    wide_hidden, last_pair, head, mean, inv = make_hidden(
        place, peers, activations, cotangent, low, high, gain, bias
    )
    other_hidden = swap_cores(wide_hidden)
    even = lax.ppermute(last_pair, TM, [(i, i + 1) for i in range(1, 15, 2)])
    odd = lax.ppermute(last_pair, TM, [(i, i + 2) for i in range(1, 15, 2)])

    head = shift(head, TM, 16, -1)

    terms, before = weight_terms(
        place, wide_hidden, other_hidden, even, odd, cotangent, other_cot
    )
    terms, head = lax.optimization_barrier((terms, head))
    arrived = lax.all_to_all(terms, CHIP_AXES, 0, 0)

    low, high, _ = lax.optimization_barrier((low, high, terms))
    pre_grad, first_grad, second_grad = backward_conv(
        place, cotangent, low, high, head, conv_weight, act, mean, inv, gain, bias
    )
    sums = per_group(first_grad, second_grad)
    parts = [lax.ppermute(sums, "x", [(i, (i + k) % 4) for i in range(4)]) for k in range(1, 4)]

    block_out = forward_conv(place, before, wide_hidden, conv_weight, act)
    block_out, parts = lax.optimization_barrier((block_out, parts))
    block_out = block_out.reshape(activations.shape)
    sums = sums + parts[0] + parts[1] + parts[2]
    other = lax.ppermute(sums, "yhi", [(0, 1), (1, 0)])
    other, arrived = lax.optimization_barrier((other, arrived))
    total = jnp.sum(arrived.astype(f32), axis=0)
    sums = sums + other
    averages = per_channel(sums / CELL_COUNT)[:, None, None, :]
    first_avg, second_avg = averages[:SLOTS], averages[SLOTS:]
    wide_inv = inv[:, None, None, :]
    centred = (activations.astype(f32) - mean[:, None, None, :]) * wide_inv
    norm_part = wide_inv * (
        pre_grad.reshape(activations.shape) - first_avg - centred * second_avg
    )
    live = (jnp.arange(SLOTS) < count)[:, None, None, None]
    input_grad = jnp.where(live, cotangent.astype(f32) + norm_part, 0.0)

    frame_total = 1 + 4 * ((16 - 1) * 3 // 2)
    grad_scale = 1.0 / math.sqrt(frame_total * 8 * ROWS * COLS)
    total = total * grad_scale
    shared = total[2 * PIECE :]
    parts = [
        jnp.concatenate(
            [total[k * PIECE : (k + 1) * PIECE], shared[:, k * 64 : (k + 1) * 64]], axis=1
        )
        for k in range(2)
    ]
    mine = jnp.where(core == 0, parts[0], parts[1])
    theirs = swap_cores(jnp.where(core == 0, parts[1], parts[0]))
    first = jnp.where(core == 0, mine, theirs)
    second = jnp.where(core == 0, theirs, mine)
    weight_grad = jnp.concatenate([first, second[:, LANES:], second[:, :LANES]], axis=1)
    return block_out, input_grad, weight_grad


def solution(mesh):
    fine = Mesh(mesh.devices.reshape(2, 4, 2, 2, 4), ALL_AXES)
    placed = P(TM, ROW_AXES, None, None)
    return jax.shard_map(
        on_device,
        mesh=fine,
        in_specs=(placed, P(), P(), P(), P(), placed),
        out_specs=(placed, placed, P(ALL_AXES, None)),
        check_vma=False,
    )
```

profile of v0, /device:TPU:1, one launch (start us, length us, event | category | flops | bytes accessed | tf_op | source)
XLA Modules:
  0.0 132.6 jit_solution(9037656335216395101)
XLA Ops:
  0.6 2.0 %local_sums.1 = f32[8,16,384]{2,1,0:T(8,128)} custom-call(bf16[8,4,32,384]{3,2,1,0:T(8,128)(2,1)} %act_ref.3), custom_call_target="tpu_custom_call" | custom-call | flops 1572864 | bytes 1048576 | tf_op jit(solution)/shard_map/local_sums/pallas_call | solution.py:412
  2.7 1.4 %collective-permute-start.2 = (bf16[8,4,32,384]{3,2,1,0:T(8,128)(2,1)}, bf16[8,4,32,384]{3,2,1,0:T(8,128)(2,1)}, u32[]{:S(2)}, u32[]{:S(2)}) collective-permute-start(bf16[8,4,32,384]{3,2,1,0:T(8,128)(2,1)} %cot_ref.5), channel_id=1, source_target_pairs={{0,8},{8,0},{1,9},{9,1},{2,10},{10,2},{3,11},{11,3},{4,12},{12,4},... | collective-permute-start | bytes 2359304 | tf_op jit(solution)/shard_map/ppermute | solution.py:505
  4.1 1.2 constant_dynamic-update-slice_fusion.1
  5.3 0.0 copy-done.1
  5.3 0.0 copy-start.5
  5.3 0.0 copy-start.6
  5.3 0.0 copy-start.4
  5.3 0.2 constant_dynamic-update-slice_fusion
  5.5 0.1 fusion.2
  5.6 1.3 collective-permute-start.1
  6.9 4.8 %collective-permute-start = (bf16[16,1,32,384]{3,2,1,0:T(8,128)(2,1)S(1)}, bf16[16,1,32,384]{3,2,1,0:T(8,128)(2,1)}, u32[]{:S(2)}, u32[]{:S(2)}) collective-permute-start(bf16[16,1,32,384]{3,2,1,0:T(8,128)(2,1)S(1)} %get-tuple-element.56), channel_id=1, source_target_pairs={{0,1},{1,2},{2,3},{3,4},{4,5},{5,6},{6,7},{8,9},{9,10},{10,11},{11... | collective-permute-start | bytes 1179656 | tf_op jit(solution)/shard_map/ppermute | solution.py:501
  11.7 6.7 %all-to-all-start = ((f32[8,16,384]{2,1,0:T(8,128)}), f32[8,16,384]{2,1,0:T(8,128)}, u32[]{:S(2)}, u32[]{:S(2)}) async-start(f32[8,16,384]{2,1,0:T(8,128)} %local_sums.1), calls=%async_computation | async-start | bytes 393216 | tf_op jit(solution)/shard_map/all_to_all | solution.py:529
  18.4 0.0 copy-done.5
  18.4 0.6 broadcast_in_dim.26.gain_ref
  19.0 0.0 copy-done.6
  19.0 0.5 broadcast_in_dim.27.bias_ref
  19.5 0.0 copy-done.4
  19.5 0.6 fusion.6
  20.1 1.8 %pad_add_fusion.place_ref = s32[4]{0:T(128)} fusion(s32[1]{0:T(128)} %get-tuple-element.66, s32[1]{0:T(128)} %bitcast.1, s32[1]{0:T(128)} %bitcast, s32[1]{0:T(128)} %get-tuple-element.65), kind=kLoop, calls=%fused_computation.15 | loop fusion | flops 12 | bytes 32 | tf_op jit(solution)/shard_map/stack | solution.py:537
  21.9 5.8 %all-to-all-done.peers_ref = f32[8,16,384]{2,1,0:T(8,128)} async-done(((f32[8,16,384]{2,1,0:T(8,128)}), f32[8,16,384]{2,1,0:T(8,128)}, u32[]{:S(2)}, u32[]{:S(2)}) %all-to-all-start) | async-done | bytes 196640 | tf_op jit(solution)/shard_map/all_to_all | solution.py:529
  27.7 0.0 collective-permute-done.1.high_ref.cot_high_ref
  27.7 0.0 collective-permute-done.low_ref.cot_low_ref
  27.7 0.0 collective-permute-done.2.other_cot_ref
  27.7 4.0 %make_hidden.1 = (bf16[8,6,32,384]{3,2,1,0:T(8,128)(2,1)}, bf16[2,6,32,384]{3,2,1,0:T(8,128)(2,1)}, bf16[2,6,32,384]{3,2,1,0:T(8,128)(2,1)}, f32[8,384]{1,0:T(8,128)}, f32[8,384]{1,0:T(8,128)}) custom-call(s32[4]{0:T(128)} %pad_add_fusion.place_ref, f32[8,16,384]{2,1,0:T(8,128)} %all-to-all-done.peers_ref, f32[384,384]{1,0:T(8,128)} %constant.41.clone.same_ref, ...), custom_call_target="tpu_custom_call" | custom-call | flops 15728640 | bytes 5242880 | tf_op jit(solution)/shard_map/make_hidden/pallas_call | solution.py:438
  31.7 1.5 %collective-permute-start.3 = (bf16[8,6,32,384]{3,2,1,0:T(8,128)(2,1)}, bf16[8,6,32,384]{3,2,1,0:T(8,128)(2,1)}, u32[]{:S(2)}, u32[]{:S(2)}) collective-permute-start(bf16[8,6,32,384]{3,2,1,0:T(8,128)(2,1)} %get-tuple-element.34.hidden_ref), channel_id=1, source_target_pairs={{0,8},{8,0},{1,9},{9,1},{2,10},{10,2},{3,11},{11,3},{4,12},{12,4},... | collective-permute-start | bytes 3538952 | tf_op jit(solution)/shard_map/ppermute | solution.py:505
  33.2 4.3 %collective-permute-start.5 = (bf16[2,6,32,384]{3,2,1,0:T(8,128)(2,1)}, bf16[2,6,32,384]{3,2,1,0:T(8,128)(2,1)}, u32[]{:S(2)}, u32[]{:S(2)}) collective-permute-start(bf16[2,6,32,384]{3,2,1,0:T(8,128)(2,1)} %get-tuple-element.35), channel_id=1, source_target_pairs={{8,24},{24,40},{40,56},{56,72},{72,88},{88,104},{104,120},{9,25},{... | collective-permute-start | bytes 884744 | tf_op jit(solution)/shard_map/ppermute | solution.py:545
  37.4 2.0 %collective-permute-start.4 = (bf16[2,6,32,384]{3,2,1,0:T(8,128)(2,1)}, bf16[2,6,32,384]{3,2,1,0:T(8,128)(2,1)}, u32[]{:S(2)}, u32[]{:S(2)}) collective-permute-start(bf16[2,6,32,384]{3,2,1,0:T(8,128)(2,1)} %get-tuple-element.35), channel_id=1, source_target_pairs={{8,16},{24,32},{40,48},{56,64},{72,80},{88,96},{104,112},{9,17},{2... | collective-permute-start | bytes 884744 | tf_op jit(solution)/shard_map/ppermute | solution.py:544
  39.4 1.9 %collective-permute-start.6 = (bf16[2,6,32,384]{3,2,1,0:T(8,128)(2,1)}, bf16[2,6,32,384]{3,2,1,0:T(8,128)(2,1)}, u32[]{:S(2)}, u32[]{:S(2)}) collective-permute-start(bf16[2,6,32,384]{3,2,1,0:T(8,128)(2,1)} %get-tuple-element.39), channel_id=1, source_target_pairs={{8,0},{16,8},{24,16},{32,24},{40,32},{48,40},{56,48},{64,56},{72,6... | collective-permute-start | bytes 884744 | tf_op jit(solution)/shard_map/ppermute | solution.py:501
  41.4 0.0 collective-permute-done.5.odd_ref
  41.4 2.5 %collective-permute-done.4.even_ref = bf16[2,6,32,384]{3,2,1,0:T(8,128)(2,1)} collective-permute-done((bf16[2,6,32,384]{3,2,1,0:T(8,128)(2,1)}, bf16[2,6,32,384]{3,2,1,0:T(8,128)(2,1)}, u32[]{:S(2)}, u32[]{:S(2)}) %collective-permute-start.4) | collective-permute-done | bytes 294944 | tf_op jit(solution)/shard_map/ppermute | solution.py:544
  43.9 0.0 collective-permute-done.3.other_ref
  43.9 16.2 %weight_terms.1 = (bf16[64,243,128]{2,1,0:T(8,128)(2,1)}, bf16[2,6,32,384]{3,2,1,0:T(8,128)(2,1)}) custom-call(s32[4]{0:T(128)} %pad_add_fusion.place_ref, bf16[8,6,32,384]{3,2,1,0:T(8,128)(2,1)} %get-tuple-element.34.hidden_ref, bf16[8,6,32,384]{3,2,1,0:T(8,128)(2,1)} %collective-permute-done.3.other_ref, ...), custom_call_target="tpu_custom_call" | custom-call | flops 8153726976 | bytes 12582912 | tf_op jit(solution)/shard_map/weight_terms/pallas_call | solution.py:477
  60.1 0.0 collective-permute-done.6.head_ref
  60.1 9.4 %all-to-all-start.1 = ((bf16[64,243,128]{2,1,0:T(8,128)(2,1)}), bf16[64,243,128]{2,1,0:T(8,128)(2,1)}, u32[]{:S(2)}, u32[]{:S(2)}) async-start(bf16[64,243,128]{2,1,0:T(8,128)(2,1)} %get-tuple-element.40), calls=%async_computation.1 | async-start | bytes 8126464 | tf_op jit(solution)/shard_map/all_to_all | solution.py:553
  69.5 17.0 %backward_conv.1 = (f32[1024,384]{1,0:T(8,128)}, f32[8,384]{1,0:T(8,128)}, f32[8,384]{1,0:T(8,128)}) custom-call(s32[4]{0:T(128)} %pad_add_fusion.place_ref, bf16[8,4,32,384]{3,2,1,0:T(8,128)(2,1)} %cot_ref.5, bf16[16,1,32,384]{3,2,1,0:T(8,128)(2,1)} %collective-permute-done.low_ref.cot_low_ref, ...), custom_call_target="tpu_custom_call" | custom-call | flops 8153726976 | bytes 12582912 | tf_op jit(solution)/shard_map/backward_conv/pallas_call | solution.py:388
  86.5 0.7 pad_maximum_fusion.3
  87.2 0.3 reshape.29
  87.5 0.7 reduce_sum.18
  88.2 2.2 %collective-permute-start.9 = (f32[16,32]{1,0:T(8,128)}, f32[16,32]{1,0:T(8,128)}, u32[]{:S(2)}, u32[]{:S(2)}) collective-permute-start(f32[16,32]{1,0:T(8,128)} %reduce_sum.18), channel_id=1, source_target_pairs={{0,3},{1,0},{2,1},{3,2},{4,7},{5,4},{6,5},{7,6},{8,11},{9,8},{10,9... | collective-permute-start | bytes 6152 | tf_op jit(solution)/shard_map/ppermute | solution.py:560
  90.4 0.6 collective-permute-start.8
  91.0 0.6 collective-permute-start.7
  91.5 15.7 %forward_conv.1 = bf16[1024,384]{1,0:T(8,128)(2,1)} custom-call(s32[4]{0:T(128)} %pad_add_fusion.place_ref, bf16[2,6,32,384]{3,2,1,0:T(8,128)(2,1)} %get-tuple-element.37.before_ref, bf16[8,6,32,384]{3,2,1,0:T(8,128)(2,1)} %get-tuple-element.34.hidden_ref, bf16[10368,384]{1,0:T(8,128)(2,1)} %w_ref.3, bf16[1024,384]{1,0:T(8,128)(2,1)} %bitcast.7), custom_call_target="tpu_custom_call" | custom-call | flops 8153726976 | bytes 12582912 | tf_op jit(solution)/shard_map/forward_conv/pallas_call | solution.py:364
  107.2 7.3 %collective-permute-done.9 = f32[16,32]{1,0:T(8,128)} collective-permute-done((f32[16,32]{1,0:T(8,128)}, f32[16,32]{1,0:T(8,128)}, u32[]{:S(2)}, u32[]{:S(2)}) %collective-permute-start.9) | collective-permute-done | bytes 2080 | tf_op jit(solution)/shard_map/ppermute | solution.py:560
  114.6 0.3 collective-permute-done.8
  114.8 0.0 collective-permute-done.7
  114.8 0.8 add_add_fusion
  115.6 3.0 %collective-permute-start.10 = (f32[16,32]{1,0:T(8,128)S(1)}, f32[16,32]{1,0:T(8,128)S(1)}, u32[]{:S(2)}, u32[]{:S(2)}) collective-permute-start(f32[16,32]{1,0:T(8,128)S(1)} %add_add_fusion), channel_id=1, source_target_pairs={{0,4},{4,0},{1,5},{5,1},{2,6},{6,2},{3,7},{7,3},{8,12},{12,8},{9,1... | collective-permute-start | bytes 6152 | tf_op jit(solution)/shard_map/ppermute | solution.py:566
  118.6 0.6 iota_compare_fusion
  119.2 1.0 collective-permute-done.10
  120.2 0.0 all-to-all-done.1
  120.2 2.9 %convert_reduce_fusion = f32[243,128]{1,0:T(8,128)S(1)} fusion(bf16[64,243,128]{2,1,0:T(8,128)(2,1)} %all-to-all-done.1), kind=kLoop, calls=%fused_computation | loop fusion | flops 3950208 | bytes 4105728 | tf_op jit(solution)/shard_map/reduce_sum | solution.py:568
  123.1 0.1 fusion.4
  123.2 0.1 broadcast_in_dim.29
  123.3 0.7 sub.25
  124.0 3.6 %collective-permute-start.11 = (f32[81,192]{1,0:T(8,128)S(1)}, f32[81,192]{1,0:T(8,128)}, u32[]{:S(2)}, u32[]{:S(2)}) collective-permute-start(f32[81,192]{1,0:T(8,128)S(1)} %fusion), channel_id=1, source_target_pairs={{0,8},{8,0},{1,9},{9,1},{2,10},{10,2},{3,11},{11,3},{4,12},{12,4},... | collective-permute-start | bytes 186632 | tf_op jit(solution)/shard_map/ppermute | solution.py:505
  127.7 0.1 broadcast_in_dim.30
  127.8 0.7 mul.48
  128.5 0.0 copy-done.2
  128.5 0.0 copy-done.3
  128.5 0.0 copy-done
  128.5 2.4 %add_select_fusion = f32[8,4,32,384]{3,2,1,0:T(8,128)} fusion(bf16[8,4,32,384]{3,2,1,0:T(8,128)(2,1)S(1)} %copy-done, f32[8,4,32,384]{3,2,1,0:T(8,128)S(1)} %bitcast.8, bf16[8,4,32,384]{3,2,1,0:T(8,128)(2,1)S(1)} %copy-done.2, f32[8,384]{1,0:T(8,128)} %mul.48, f32[8,384]{1,0:T(8,128)} %get-tuple-element.44.mean_ref, f32[8,384]{1,0:T(8,128)} %sub.25, ...), kind=kLoop, calls=%fused_computation.1 | loop fusion | flops 3932160 | bytes 4767752 | tf_op jit(solution)/shard_map/jit(_where)/select_n | solution.py:578
  130.9 0.0 collective-permute-done.11
  130.9 0.9 broadcast_select_fusion.1
  131.9 0.8 pad_maximum_fusion
  (11 shorter events, 0.1 us)
Async XLA Ops:
  2.6 2.7 %copy-start.1 = (bf16[8,4,32,384]{3,2,1,0:T(8,128)(2,1)S(1)}, bf16[8,4,32,384]{3,2,1,0:T(8,128)(2,1)}, u32[]{:S(2)}) copy-start(bf16[8,4,32,384]{3,2,1,0:T(8,128)(2,1)} %cot_ref.5) | copy-start | bytes 2359300
  2.7 25.0 %collective-permute-start.2 = (bf16[8,4,32,384]{3,2,1,0:T(8,128)(2,1)}, bf16[8,4,32,384]{3,2,1,0:T(8,128)(2,1)}, u32[]{:S(2)}, u32[]{:S(2)}) collective-permute-start(bf16[8,4,32,384]{3,2,1,0:T(8,128)(2,1)} %cot_ref.5), channel_id=1, source_target_pairs={{0,8},{8,0},{1,9},{9,1},{2,10},{10,2},{3,11},{11,3},{4,12},{12,4},... | collective-permute-start | bytes 2359304 | tf_op jit(solution)/shard_map/ppermute | solution.py:505
  5.3 13.1 %copy-start.5 = (f32[384]{0:T(512)S(1)}, f32[384]{0:T(512)}, u32[]{:S(2)}) copy-start(f32[384]{0:T(512)} %param.9) | copy-start | bytes 4612
  5.3 13.7 %copy-start.6 = (f32[384]{0:T(512)S(1)}, f32[384]{0:T(512)}, u32[]{:S(2)}) copy-start(f32[384]{0:T(512)} %param.10) | copy-start | bytes 4612
  5.3 14.2 %copy-start.4 = (s32[16]{0:T(128)S(1)}, s32[16]{0:T(128)}, u32[]{:S(2)}) copy-start(s32[16]{0:T(128)} %param.8) | copy-start | bytes 196
  5.6 22.1 %collective-permute-start.1 = (bf16[16,1,32,384]{3,2,1,0:T(8,128)(2,1)S(1)}, bf16[16,1,32,384]{3,2,1,0:T(8,128)(2,1)}, u32[]{:S(2)}, u32[]{:S(2)}) collective-permute-start(bf16[16,1,32,384]{3,2,1,0:T(8,128)(2,1)S(1)} %get-tuple-element.55), channel_id=1, source_target_pairs={{1,0},{2,1},{3,2},{4,3},{5,4},{6,5},{7,6},{9,8},{10,9},{11,10},{12... | collective-permute-start | bytes 1179656 | tf_op jit(solution)/shard_map/ppermute | solution.py:501
  6.9 20.8 %collective-permute-start = (bf16[16,1,32,384]{3,2,1,0:T(8,128)(2,1)S(1)}, bf16[16,1,32,384]{3,2,1,0:T(8,128)(2,1)}, u32[]{:S(2)}, u32[]{:S(2)}) collective-permute-start(bf16[16,1,32,384]{3,2,1,0:T(8,128)(2,1)S(1)} %get-tuple-element.56), channel_id=1, source_target_pairs={{0,1},{1,2},{2,3},{3,4},{4,5},{5,6},{6,7},{8,9},{9,10},{10,11},{11... | collective-permute-start | bytes 1179656 | tf_op jit(solution)/shard_map/ppermute | solution.py:501
  11.7 16.0 %all-to-all-start = ((f32[8,16,384]{2,1,0:T(8,128)}), f32[8,16,384]{2,1,0:T(8,128)}, u32[]{:S(2)}, u32[]{:S(2)}) async-start(f32[8,16,384]{2,1,0:T(8,128)} %local_sums.1), calls=%async_computation | async-start | bytes 393216 | tf_op jit(solution)/shard_map/all_to_all | solution.py:529
  31.7 12.2 %collective-permute-start.3 = (bf16[8,6,32,384]{3,2,1,0:T(8,128)(2,1)}, bf16[8,6,32,384]{3,2,1,0:T(8,128)(2,1)}, u32[]{:S(2)}, u32[]{:S(2)}) collective-permute-start(bf16[8,6,32,384]{3,2,1,0:T(8,128)(2,1)} %get-tuple-element.34.hidden_ref), channel_id=1, source_target_pairs={{0,8},{8,0},{1,9},{9,1},{2,10},{10,2},{3,11},{11,3},{4,12},{12,4},... | collective-permute-start | bytes 3538952 | tf_op jit(solution)/shard_map/ppermute | solution.py:505
  33.2 8.2 %collective-permute-start.5 = (bf16[2,6,32,384]{3,2,1,0:T(8,128)(2,1)}, bf16[2,6,32,384]{3,2,1,0:T(8,128)(2,1)}, u32[]{:S(2)}, u32[]{:S(2)}) collective-permute-start(bf16[2,6,32,384]{3,2,1,0:T(8,128)(2,1)} %get-tuple-element.35), channel_id=1, source_target_pairs={{8,24},{24,40},{40,56},{56,72},{72,88},{88,104},{104,120},{9,25},{... | collective-permute-start | bytes 884744 | tf_op jit(solution)/shard_map/ppermute | solution.py:545
  37.4 6.4 %collective-permute-start.4 = (bf16[2,6,32,384]{3,2,1,0:T(8,128)(2,1)}, bf16[2,6,32,384]{3,2,1,0:T(8,128)(2,1)}, u32[]{:S(2)}, u32[]{:S(2)}) collective-permute-start(bf16[2,6,32,384]{3,2,1,0:T(8,128)(2,1)} %get-tuple-element.35), channel_id=1, source_target_pairs={{8,16},{24,32},{40,48},{56,64},{72,80},{88,96},{104,112},{9,17},{2... | collective-permute-start | bytes 884744 | tf_op jit(solution)/shard_map/ppermute | solution.py:544
  39.4 20.6 %collective-permute-start.6 = (bf16[2,6,32,384]{3,2,1,0:T(8,128)(2,1)}, bf16[2,6,32,384]{3,2,1,0:T(8,128)(2,1)}, u32[]{:S(2)}, u32[]{:S(2)}) collective-permute-start(bf16[2,6,32,384]{3,2,1,0:T(8,128)(2,1)} %get-tuple-element.39), channel_id=1, source_target_pairs={{8,0},{16,8},{24,16},{32,24},{40,32},{48,40},{56,48},{64,56},{72,6... | collective-permute-start | bytes 884744 | tf_op jit(solution)/shard_map/ppermute | solution.py:501
  60.1 60.1 %all-to-all-start.1 = ((bf16[64,243,128]{2,1,0:T(8,128)(2,1)}), bf16[64,243,128]{2,1,0:T(8,128)(2,1)}, u32[]{:S(2)}, u32[]{:S(2)}) async-start(bf16[64,243,128]{2,1,0:T(8,128)(2,1)} %get-tuple-element.40), calls=%async_computation.1 | async-start | bytes 8126464 | tf_op jit(solution)/shard_map/all_to_all | solution.py:553
  88.2 26.3 %collective-permute-start.9 = (f32[16,32]{1,0:T(8,128)}, f32[16,32]{1,0:T(8,128)}, u32[]{:S(2)}, u32[]{:S(2)}) collective-permute-start(f32[16,32]{1,0:T(8,128)} %reduce_sum.18), channel_id=1, source_target_pairs={{0,3},{1,0},{2,1},{3,2},{4,7},{5,4},{6,5},{7,6},{8,11},{9,8},{10,9... | collective-permute-start | bytes 6152 | tf_op jit(solution)/shard_map/ppermute | solution.py:560
  90.4 24.4 %collective-permute-start.8 = (f32[16,32]{1,0:T(8,128)}, f32[16,32]{1,0:T(8,128)}, u32[]{:S(2)}, u32[]{:S(2)}) collective-permute-start(f32[16,32]{1,0:T(8,128)} %reduce_sum.18), channel_id=1, source_target_pairs={{0,2},{1,3},{2,0},{3,1},{4,6},{5,7},{6,4},{7,5},{8,10},{9,11},{10,... | collective-permute-start | bytes 6152 | tf_op jit(solution)/shard_map/ppermute | solution.py:560
  91.0 23.9 %collective-permute-start.7 = (f32[16,32]{1,0:T(8,128)}, f32[16,32]{1,0:T(8,128)}, u32[]{:S(2)}, u32[]{:S(2)}) collective-permute-start(f32[16,32]{1,0:T(8,128)} %reduce_sum.18), channel_id=1, source_target_pairs={{0,1},{1,2},{2,3},{3,0},{4,5},{5,6},{6,7},{7,4},{8,9},{9,10},{10,1... | collective-permute-start | bytes 6152 | tf_op jit(solution)/shard_map/ppermute | solution.py:560
  115.6 4.6 %collective-permute-start.10 = (f32[16,32]{1,0:T(8,128)S(1)}, f32[16,32]{1,0:T(8,128)S(1)}, u32[]{:S(2)}, u32[]{:S(2)}) collective-permute-start(f32[16,32]{1,0:T(8,128)S(1)} %add_add_fusion), channel_id=1, source_target_pairs={{0,4},{4,0},{1,5},{5,1},{2,6},{6,2},{3,7},{7,3},{8,12},{12,8},{9,1... | collective-permute-start | bytes 6152 | tf_op jit(solution)/shard_map/ppermute | solution.py:566
  120.2 8.3 %copy-start.2 = (bf16[8,4,32,384]{3,2,1,0:T(8,128)(2,1)S(1)}, bf16[8,4,32,384]{3,2,1,0:T(8,128)(2,1)}, u32[]{:S(2)}) copy-start(bf16[8,4,32,384]{3,2,1,0:T(8,128)(2,1)} %cot_ref.5) | copy-start | bytes 2359300
  120.2 8.3 %copy-start.3 = (f32[1024,384]{1,0:T(8,128)S(1)}, f32[1024,384]{1,0:T(8,128)}, u32[]{:S(2)}) copy-start(f32[1024,384]{1,0:T(8,128)} %get-tuple-element.49) | copy-start | bytes 4718596
  123.1 5.4 %copy-start = (bf16[8,4,32,384]{3,2,1,0:T(8,128)(2,1)S(1)}, bf16[8,4,32,384]{3,2,1,0:T(8,128)(2,1)}, u32[]{:S(2)}) copy-start(bf16[8,4,32,384]{3,2,1,0:T(8,128)(2,1)} %act_ref.3) | copy-start | bytes 2359300
  124.0 6.9 %collective-permute-start.11 = (f32[81,192]{1,0:T(8,128)S(1)}, f32[81,192]{1,0:T(8,128)}, u32[]{:S(2)}, u32[]{:S(2)}) collective-permute-start(f32[81,192]{1,0:T(8,128)S(1)} %fusion), channel_id=1, source_target_pairs={{0,8},{8,0},{1,9},{9,1},{2,10},{10,2},{3,11},{11,3},{4,12},{12,4},... | collective-permute-start | bytes 186632 | tf_op jit(solution)/shard_map/ppermute | solution.py:505
where the time goes:
time: 133 us
  Pallas kernels  54.9 us (41%)
  starting transfers between devices  43.2 us (32%)
  waiting for transfers between devices  16.9 us (13%)
  other arithmetic  11.6 us (9%)
  local copies, waits for them, and re-layouts  5.18 us (4%)
    pallas_call x1, Pallas kernels, backward_conv(): pl.pallas_call(backward_kernel, out_shape=(jax.ShapeDtypeStruct((POS, CHA...  17 us
    pallas_call x1, Pallas kernels, weight_terms(): pl.pallas_call(weight_kernel, out_shape=(jax.ShapeDtypeStruct((CHIPS, 3 *...  16.2 us
    pallas_call x1, Pallas kernels, forward_conv(): pl.pallas_call(forward_kernel, out_shape=jax.ShapeDtypeStruct((POS, CHAN)...  15.7 us
    all_to_all x1, starting transfers between devices, on_device(): arrived = lax.all_to_all(terms, CHIP_AXES, 0, 0)  9.4 us
    ppermute x3, starting transfers between devices, shift(): return lax.ppermute(values, axes, pairs)  7.98 us
    ppermute x3, waiting for transfers between devices, on_device(): lax.ppermute(sums, 'x', [(i, (i + k) % 4) for i in range(4)])  7.62 us
    all_to_all x1, starting transfers between devices, on_device(): peers = lax.all_to_all(sums, ROW_AXES, 0, 0)  6.71 us
    ppermute x3, starting transfers between devices, swap_cores(): return lax.ppermute(values, 'core', [(0, 1), (1, 0)])  6.58 us
  transfers between devices with their start and end apart: 14, of which 5 were waited for; matrix products, arithmetic and copies ran while one was open for 8% of the time, Pallas kernels for 37%

commit v1 on v0

--- a/solution.py
+++ b/solution.py
@@ -274,7 +274,7 @@
         copy.wait()
 
 
-def sums_kernel(act_ref, out_ref):
+def sums_kernel(act_ref, cot_ref, out_ref, bottom_ref, top_ref):
     firsts, seconds = [], []
     for frame in range(SLOTS):
         values = act_ref[frame].reshape(CELLS, CHAN).astype(f32)
@@ -283,6 +283,9 @@
     both = jnp.concatenate(firsts + seconds, axis=0)
     for peer in range(8):
         out_ref[peer] = both
+    for first, ref in ((0, act_ref), (SLOTS, cot_ref)):
+        bottom_ref[first : first + SLOTS] = ref[:, ROWS - 1 :]
+        top_ref[first : first + SLOTS] = ref[:, :1]
 
 
 def group_means(sums, same_ref):
@@ -408,14 +411,15 @@
     )(place, cot, low, high, head, weights, act, *smalls)
 
 
-def local_sums(act):
+def local_sums(act, cot):
+    edge = jax.ShapeDtypeStruct((2 * SLOTS, 1, COLS, CHAN), bf16)
     return pl.pallas_call(
         sums_kernel,
-        out_shape=jax.ShapeDtypeStruct((8, 2 * SLOTS, CHAN), f32),
+        out_shape=(jax.ShapeDtypeStruct((8, 2 * SLOTS, CHAN), f32), edge, edge),
         compiler_params=VMEM_LIMIT,
-        cost_estimate=cost(4 * POS * CHAN, 1 << 20),
+        cost_estimate=cost(4 * POS * CHAN, 3 << 20),
         name="local_sums",
-    )(act)
+    )(act, cot)
 
 
 SMEM_SPEC = pl.BlockSpec(memory_space=pltpu.SMEM)
@@ -505,12 +509,6 @@
     return lax.ppermute(values, "core", [(0, 1), (1, 0)])
 
 
-def edge_rows(block):
-    low = shift(block[:, ROWS - 1 :], ROW_AXES, 8, 1)
-    high = shift(block[:, :1], ROW_AXES, 8, -1)
-    return low, high
-
-
 def per_group(first, second):
     grouped = jnp.concatenate([first, second], axis=0).reshape(2 * SLOTS, GROUPS, CHAN // GROUPS)
     return jnp.sum(grouped, axis=2)
@@ -525,11 +523,11 @@
     act = activations.reshape(POS, CHAN)
     gain, bias = norm_gain[None], norm_bias[None]
 
-    sums = local_sums(activations)
+    sums, bottom, top = local_sums(activations, cotangent)
     peers = lax.all_to_all(sums, ROW_AXES, 0, 0)
-    source, rows_at_once, _ = lax.optimization_barrier((activations, cotangent, sums))
-    low, high = edge_rows(jnp.concatenate([source, rows_at_once], 0))
-    other_cot = swap_cores(rows_at_once)
+    low = shift(bottom, ROW_AXES, 8, 1)
+    high = shift(top, ROW_AXES, 8, -1)
+    other_cot = swap_cores(cotangent)
     low, high, peers, other_cot = lax.optimization_barrier((low, high, peers, other_cot))
 
     tm = lax.axis_index(TM)

time: 133 us -> 132 us (level)
  waiting for transfers between devices: 16.9 us -> 13.1 us
    all_to_all x1, waiting for transfers between devices: 5.77 us -> 1.98 us  [on_device(): peers = lax.all_to_all(sums, ROW_AXES, 0, 0)]
  transfers between devices with their start and end apart: 14 -> 14, of which waited for: 5 -> 5; matrix products, arithmetic and copies ran while one was open for 8% -> 9% of each run, Pallas kernels for 37% -> 39%
where the time goes in v1:
time: 132 us; the launch traced here: 131 us
  Pallas kernels  55.3 us (42%)
  starting transfers between devices  44.4 us (34%)
  waiting for transfers between devices  13.1 us (10%)
  other arithmetic  11.7 us (9%)
  local copies, waits for them, and re-layouts  5.76 us (4%)
    pallas_call x1, Pallas kernels, backward_conv(): pl.pallas_call(backward_kernel, out_shape=(jax.ShapeDtypeStruct((POS, CHA...  17 us
    pallas_call x1, Pallas kernels, weight_terms(): pl.pallas_call(weight_kernel, out_shape=(jax.ShapeDtypeStruct((CHIPS, 3 *...  16.2 us
    pallas_call x1, Pallas kernels, forward_conv(): pl.pallas_call(forward_kernel, out_shape=jax.ShapeDtypeStruct((POS, CHAN)...  15.7 us
    all_to_all x1, starting transfers between devices, on_device(): arrived = lax.all_to_all(terms, CHIP_AXES, 0, 0)  9.83 us
    all_to_all x1, starting transfers between devices, on_device(): peers = lax.all_to_all(sums, ROW_AXES, 0, 0)  7.95 us
    ppermute x3, waiting for transfers between devices, on_device(): lax.ppermute(sums, 'x', [(i, (i + k) % 4) for i in range(4)])  7.61 us
    ppermute x3, starting transfers between devices, shift(): return lax.ppermute(values, axes, pairs)  7.14 us
    ppermute x3, starting transfers between devices, swap_cores(): return lax.ppermute(values, 'core', [(0, 1), (1, 0)])  6.96 us
  transfers between devices with their start and end apart: 14, of which 5 were waited for; matrix products, arithmetic and copies ran while one was open for 9% of the time, Pallas kernels for 39%

profile of v1, /device:TPU:1, one launch (start us, length us, event | category | flops | bytes accessed | tf_op | source)
XLA Modules:
  0.0 131.1 jit_solution(13915162290182399654)
XLA Ops:
  0.6 1.5 %collective-permute-start.2 = (bf16[8,4,32,384]{3,2,1,0:T(8,128)(2,1)}, bf16[8,4,32,384]{3,2,1,0:T(8,128)(2,1)}, u32[]{:S(2)}, u32[]{:S(2)}) collective-permute-start(bf16[8,4,32,384]{3,2,1,0:T(8,128)(2,1)} %cot_ref.7), channel_id=1, source_target_pairs={{0,8},{8,0},{1,9},{9,1},{2,10},{10,2},{3,11},{11,3},{4,12},{12,4},... | collective-permute-start | bytes 2359304 | tf_op jit(solution)/shard_map/ppermute | solution.py:509
  2.1 2.5 %local_sums.1 = (f32[8,16,384]{2,1,0:T(8,128)}, bf16[16,1,32,384]{3,2,1,0:T(8,128)(2,1)}, bf16[16,1,32,384]{3,2,1,0:T(8,128)(2,1)}) custom-call(bf16[8,4,32,384]{3,2,1,0:T(8,128)(2,1)} %act_ref.3, bf16[8,4,32,384]{3,2,1,0:T(8,128)(2,1)} %cot_ref.7), custom_call_target="tpu_custom_call" | custom-call | flops 1572864 | bytes 3145728 | tf_op jit(solution)/shard_map/local_sums/pallas_call | solution.py:416
  4.6 4.0 %collective-permute-start = (bf16[16,1,32,384]{3,2,1,0:T(8,128)(2,1)}, bf16[16,1,32,384]{3,2,1,0:T(8,128)(2,1)}, u32[]{:S(2)}, u32[]{:S(2)}) collective-permute-start(bf16[16,1,32,384]{3,2,1,0:T(8,128)(2,1)} %get-tuple-element.30), channel_id=1, source_target_pairs={{0,1},{1,2},{2,3},{3,4},{4,5},{5,6},{6,7},{8,9},{9,10},{10,11},{11... | collective-permute-start | bytes 1179656 | tf_op jit(solution)/shard_map/ppermute | solution.py:505
  8.6 1.3 collective-permute-start.1
  9.8 7.9 %all-to-all-start = ((f32[8,16,384]{2,1,0:T(8,128)}), f32[8,16,384]{2,1,0:T(8,128)}, u32[]{:S(2)}, u32[]{:S(2)}) async-start(f32[8,16,384]{2,1,0:T(8,128)} %get-tuple-element.32), calls=%async_computation | async-start | bytes 393216 | tf_op jit(solution)/shard_map/all_to_all | solution.py:527
  17.8 1.2 broadcast_in_dim.26.gain_ref
  19.0 1.2 broadcast_in_dim.27.bias_ref
  20.2 1.3 %fusion.5 = (s32[1]{0:T(128)}, s32[1]{0:T(128)}) fusion(s32[16]{0:T(128)} %param.8, s32[]{:T(128)S(6)} %select_n.30, s32[]{:T(128)S(6)} %select_n.31), kind=kLoop, calls=%fused_computation.18 | loop fusion | bytes 24 | tf_op jit(solution)/shard_map/dynamic_slice | solution.py:534
  21.6 1.9 %pad_add_fusion.place_ref = s32[4]{0:T(128)} fusion(s32[1]{0:T(128)} %get-tuple-element.66, s32[1]{0:T(128)} %bitcast.1, s32[1]{0:T(128)} %bitcast, s32[1]{0:T(128)} %get-tuple-element.65), kind=kLoop, calls=%fused_computation.13 | loop fusion | flops 12 | bytes 32 | tf_op jit(solution)/shard_map/stack | solution.py:535
  23.5 2.0 %all-to-all-done.peers_ref = f32[8,16,384]{2,1,0:T(8,128)} async-done(((f32[8,16,384]{2,1,0:T(8,128)}), f32[8,16,384]{2,1,0:T(8,128)}, u32[]{:S(2)}, u32[]{:S(2)}) %all-to-all-start) | async-done | bytes 196640 | tf_op jit(solution)/shard_map/all_to_all | solution.py:527
  25.4 0.0 collective-permute-done.low_ref.cot_low_ref
  25.5 0.0 collective-permute-done.1.high_ref.cot_high_ref
  25.5 0.0 collective-permute-done.2.other_cot_ref
  25.5 4.0 %make_hidden.1 = (bf16[8,6,32,384]{3,2,1,0:T(8,128)(2,1)}, bf16[2,6,32,384]{3,2,1,0:T(8,128)(2,1)}, bf16[2,6,32,384]{3,2,1,0:T(8,128)(2,1)}, f32[8,384]{1,0:T(8,128)}, f32[8,384]{1,0:T(8,128)}) custom-call(s32[4]{0:T(128)} %pad_add_fusion.place_ref, f32[8,16,384]{2,1,0:T(8,128)} %all-to-all-done.peers_ref, f32[384,384]{1,0:T(8,128)} %constant.41.clone.same_ref, ...), custom_call_target="tpu_custom_call" | custom-call | flops 15728640 | bytes 5242880 | tf_op jit(solution)/shard_map/make_hidden/pallas_call | solution.py:442
  29.4 1.8 %collective-permute-start.3 = (bf16[8,6,32,384]{3,2,1,0:T(8,128)(2,1)}, bf16[8,6,32,384]{3,2,1,0:T(8,128)(2,1)}, u32[]{:S(2)}, u32[]{:S(2)}) collective-permute-start(bf16[8,6,32,384]{3,2,1,0:T(8,128)(2,1)} %get-tuple-element.36.hidden_ref), channel_id=1, source_target_pairs={{0,8},{8,0},{1,9},{9,1},{2,10},{10,2},{3,11},{11,3},{4,12},{12,4},... | collective-permute-start | bytes 3538952 | tf_op jit(solution)/shard_map/ppermute | solution.py:509
  31.2 4.3 %collective-permute-start.5 = (bf16[2,6,32,384]{3,2,1,0:T(8,128)(2,1)}, bf16[2,6,32,384]{3,2,1,0:T(8,128)(2,1)}, u32[]{:S(2)}, u32[]{:S(2)}) collective-permute-start(bf16[2,6,32,384]{3,2,1,0:T(8,128)(2,1)} %get-tuple-element.37), channel_id=1, source_target_pairs={{8,24},{24,40},{40,56},{56,72},{72,88},{88,104},{104,120},{9,25},{... | collective-permute-start | bytes 884744 | tf_op jit(solution)/shard_map/ppermute | solution.py:543
  35.5 2.0 %collective-permute-start.4 = (bf16[2,6,32,384]{3,2,1,0:T(8,128)(2,1)}, bf16[2,6,32,384]{3,2,1,0:T(8,128)(2,1)}, u32[]{:S(2)}, u32[]{:S(2)}) collective-permute-start(bf16[2,6,32,384]{3,2,1,0:T(8,128)(2,1)} %get-tuple-element.37), channel_id=1, source_target_pairs={{8,16},{24,32},{40,48},{56,64},{72,80},{88,96},{104,112},{9,17},{2... | collective-permute-start | bytes 884744 | tf_op jit(solution)/shard_map/ppermute | solution.py:542
  37.5 1.9 %collective-permute-start.6 = (bf16[2,6,32,384]{3,2,1,0:T(8,128)(2,1)}, bf16[2,6,32,384]{3,2,1,0:T(8,128)(2,1)}, u32[]{:S(2)}, u32[]{:S(2)}) collective-permute-start(bf16[2,6,32,384]{3,2,1,0:T(8,128)(2,1)} %get-tuple-element.41), channel_id=1, source_target_pairs={{8,0},{16,8},{24,16},{32,24},{40,32},{48,40},{56,48},{64,56},{72,6... | collective-permute-start | bytes 884744 | tf_op jit(solution)/shard_map/ppermute | solution.py:505
  39.4 0.0 collective-permute-done.5.odd_ref
  39.4 2.5 %collective-permute-done.4.even_ref = bf16[2,6,32,384]{3,2,1,0:T(8,128)(2,1)} collective-permute-done((bf16[2,6,32,384]{3,2,1,0:T(8,128)(2,1)}, bf16[2,6,32,384]{3,2,1,0:T(8,128)(2,1)}, u32[]{:S(2)}, u32[]{:S(2)}) %collective-permute-start.4) | collective-permute-done | bytes 294944 | tf_op jit(solution)/shard_map/ppermute | solution.py:542
  41.9 0.0 collective-permute-done.3.other_ref
  41.9 16.2 %weight_terms.1 = (bf16[64,243,128]{2,1,0:T(8,128)(2,1)}, bf16[2,6,32,384]{3,2,1,0:T(8,128)(2,1)}) custom-call(s32[4]{0:T(128)} %pad_add_fusion.place_ref, bf16[8,6,32,384]{3,2,1,0:T(8,128)(2,1)} %get-tuple-element.36.hidden_ref, bf16[8,6,32,384]{3,2,1,0:T(8,128)(2,1)} %collective-permute-done.3.other_ref, ...), custom_call_target="tpu_custom_call" | custom-call | flops 8153726976 | bytes 12582912 | tf_op jit(solution)/shard_map/weight_terms/pallas_call | solution.py:481
  58.1 0.0 collective-permute-done.6.head_ref
  58.2 9.8 %all-to-all-start.1 = ((bf16[64,243,128]{2,1,0:T(8,128)(2,1)}), bf16[64,243,128]{2,1,0:T(8,128)(2,1)}, u32[]{:S(2)}, u32[]{:S(2)}) async-start(bf16[64,243,128]{2,1,0:T(8,128)(2,1)} %get-tuple-element.42), calls=%async_computation.1 | async-start | bytes 8126464 | tf_op jit(solution)/shard_map/all_to_all | solution.py:551
  68.0 17.0 %backward_conv.1 = (f32[1024,384]{1,0:T(8,128)}, f32[8,384]{1,0:T(8,128)}, f32[8,384]{1,0:T(8,128)}) custom-call(s32[4]{0:T(128)} %pad_add_fusion.place_ref, bf16[8,4,32,384]{3,2,1,0:T(8,128)(2,1)} %cot_ref.7, bf16[16,1,32,384]{3,2,1,0:T(8,128)(2,1)} %collective-permute-done.low_ref.cot_low_ref, ...), custom_call_target="tpu_custom_call" | custom-call | flops 8153726976 | bytes 12582912 | tf_op jit(solution)/shard_map/backward_conv/pallas_call | solution.py:391
  85.0 0.7 pad_maximum_fusion.3
  85.7 0.3 reshape.29
  86.0 0.7 reduce_sum.18
  86.7 2.2 %collective-permute-start.9 = (f32[16,32]{1,0:T(8,128)}, f32[16,32]{1,0:T(8,128)}, u32[]{:S(2)}, u32[]{:S(2)}) collective-permute-start(f32[16,32]{1,0:T(8,128)} %reduce_sum.18), channel_id=1, source_target_pairs={{0,3},{1,0},{2,1},{3,2},{4,7},{5,4},{6,5},{7,6},{8,11},{9,8},{10,9... | collective-permute-start | bytes 6152 | tf_op jit(solution)/shard_map/ppermute | solution.py:558
  88.9 0.6 collective-permute-start.8
  89.5 0.6 collective-permute-start.7
  90.0 15.7 %forward_conv.1 = bf16[1024,384]{1,0:T(8,128)(2,1)} custom-call(s32[4]{0:T(128)} %pad_add_fusion.place_ref, bf16[2,6,32,384]{3,2,1,0:T(8,128)(2,1)} %get-tuple-element.39.before_ref, bf16[8,6,32,384]{3,2,1,0:T(8,128)(2,1)} %get-tuple-element.36.hidden_ref, bf16[10368,384]{1,0:T(8,128)(2,1)} %w_ref.3, bf16[1024,384]{1,0:T(8,128)(2,1)} %bitcast.7), custom_call_target="tpu_custom_call" | custom-call | flops 8153726976 | bytes 12582912 | tf_op jit(solution)/shard_map/forward_conv/pallas_call | solution.py:367
  105.7 7.3 %collective-permute-done.9 = f32[16,32]{1,0:T(8,128)} collective-permute-done((f32[16,32]{1,0:T(8,128)}, f32[16,32]{1,0:T(8,128)}, u32[]{:S(2)}, u32[]{:S(2)}) %collective-permute-start.9) | collective-permute-done | bytes 2080 | tf_op jit(solution)/shard_map/ppermute | solution.py:558
  113.0 0.3 collective-permute-done.8
  113.3 0.0 collective-permute-done.7
  113.3 0.8 add_add_fusion
  114.1 3.0 %collective-permute-start.10 = (f32[16,32]{1,0:T(8,128)S(1)}, f32[16,32]{1,0:T(8,128)S(1)}, u32[]{:S(2)}, u32[]{:S(2)}) collective-permute-start(f32[16,32]{1,0:T(8,128)S(1)} %add_add_fusion), channel_id=1, source_target_pairs={{0,4},{4,0},{1,5},{5,1},{2,6},{6,2},{3,7},{7,3},{8,12},{12,8},{9,1... | collective-permute-start | bytes 6152 | tf_op jit(solution)/shard_map/ppermute | solution.py:564
  117.1 0.6 iota_compare_fusion
  117.7 1.0 collective-permute-done.10
  118.7 0.0 all-to-all-done.1
  118.7 0.0 copy-start.1
  118.7 0.0 copy-start.2
  118.7 2.9 %convert_reduce_fusion = f32[243,128]{1,0:T(8,128)S(1)} fusion(bf16[64,243,128]{2,1,0:T(8,128)(2,1)} %all-to-all-done.1), kind=kLoop, calls=%fused_computation | loop fusion | flops 3950208 | bytes 4105728 | tf_op jit(solution)/shard_map/reduce_sum | solution.py:566
  121.6 0.0 copy-start
  121.6 0.1 fusion.3
  121.7 0.1 broadcast_in_dim.29
  121.8 0.7 sub.25
  122.5 3.6 %collective-permute-start.11 = (f32[81,192]{1,0:T(8,128)S(1)}, f32[81,192]{1,0:T(8,128)}, u32[]{:S(2)}, u32[]{:S(2)}) collective-permute-start(f32[81,192]{1,0:T(8,128)S(1)} %fusion), channel_id=1, source_target_pairs={{0,8},{8,0},{1,9},{9,1},{2,10},{10,2},{3,11},{11,3},{4,12},{12,4},... | collective-permute-start | bytes 186632 | tf_op jit(solution)/shard_map/ppermute | solution.py:509
  126.2 0.1 broadcast_in_dim.30
  126.3 0.7 mul.48
  127.0 0.0 copy-done.1
  127.0 0.0 copy-done.2
  127.0 0.0 copy-done
  127.0 2.4 %add_select_fusion = f32[8,4,32,384]{3,2,1,0:T(8,128)} fusion(bf16[8,4,32,384]{3,2,1,0:T(8,128)(2,1)S(1)} %copy-done, f32[8,4,32,384]{3,2,1,0:T(8,128)S(1)} %bitcast.8, bf16[8,4,32,384]{3,2,1,0:T(8,128)(2,1)S(1)} %copy-done.1, f32[8,384]{1,0:T(8,128)} %mul.48, f32[8,384]{1,0:T(8,128)} %get-tuple-element.46.mean_ref, f32[8,384]{1,0:T(8,128)} %sub.25, ...), kind=kLoop, calls=%fused_computation.1 | loop fusion | flops 3932160 | bytes 4767752 | tf_op jit(solution)/shard_map/jit(_where)/select_n | solution.py:576
  129.4 0.0 collective-permute-done.11
  129.4 0.9 broadcast_select_fusion.1
  130.4 0.8 pad_maximum_fusion
  (7 shorter events, 0.1 us)
Async XLA Ops:
  0.6 24.8 %collective-permute-start.2 = (bf16[8,4,32,384]{3,2,1,0:T(8,128)(2,1)}, bf16[8,4,32,384]{3,2,1,0:T(8,128)(2,1)}, u32[]{:S(2)}, u32[]{:S(2)}) collective-permute-start(bf16[8,4,32,384]{3,2,1,0:T(8,128)(2,1)} %cot_ref.7), channel_id=1, source_target_pairs={{0,8},{8,0},{1,9},{9,1},{2,10},{10,2},{3,11},{11,3},{4,12},{12,4},... | collective-permute-start | bytes 2359304 | tf_op jit(solution)/shard_map/ppermute | solution.py:509
  4.6 20.9 %collective-permute-start = (bf16[16,1,32,384]{3,2,1,0:T(8,128)(2,1)}, bf16[16,1,32,384]{3,2,1,0:T(8,128)(2,1)}, u32[]{:S(2)}, u32[]{:S(2)}) collective-permute-start(bf16[16,1,32,384]{3,2,1,0:T(8,128)(2,1)} %get-tuple-element.30), channel_id=1, source_target_pairs={{0,1},{1,2},{2,3},{3,4},{4,5},{5,6},{6,7},{8,9},{9,10},{10,11},{11... | collective-permute-start | bytes 1179656 | tf_op jit(solution)/shard_map/ppermute | solution.py:505
  8.6 16.9 %collective-permute-start.1 = (bf16[16,1,32,384]{3,2,1,0:T(8,128)(2,1)}, bf16[16,1,32,384]{3,2,1,0:T(8,128)(2,1)}, u32[]{:S(2)}, u32[]{:S(2)}) collective-permute-start(bf16[16,1,32,384]{3,2,1,0:T(8,128)(2,1)} %get-tuple-element.31), channel_id=1, source_target_pairs={{1,0},{2,1},{3,2},{4,3},{5,4},{6,5},{7,6},{9,8},{10,9},{11,10},{12... | collective-permute-start | bytes 1179656 | tf_op jit(solution)/shard_map/ppermute | solution.py:505
  9.8 15.6 %all-to-all-start = ((f32[8,16,384]{2,1,0:T(8,128)}), f32[8,16,384]{2,1,0:T(8,128)}, u32[]{:S(2)}, u32[]{:S(2)}) async-start(f32[8,16,384]{2,1,0:T(8,128)} %get-tuple-element.32), calls=%async_computation | async-start | bytes 393216 | tf_op jit(solution)/shard_map/all_to_all | solution.py:527
  29.4 12.5 %collective-permute-start.3 = (bf16[8,6,32,384]{3,2,1,0:T(8,128)(2,1)}, bf16[8,6,32,384]{3,2,1,0:T(8,128)(2,1)}, u32[]{:S(2)}, u32[]{:S(2)}) collective-permute-start(bf16[8,6,32,384]{3,2,1,0:T(8,128)(2,1)} %get-tuple-element.36.hidden_ref), channel_id=1, source_target_pairs={{0,8},{8,0},{1,9},{9,1},{2,10},{10,2},{3,11},{11,3},{4,12},{12,4},... | collective-permute-start | bytes 3538952 | tf_op jit(solution)/shard_map/ppermute | solution.py:509
  31.2 8.2 %collective-permute-start.5 = (bf16[2,6,32,384]{3,2,1,0:T(8,128)(2,1)}, bf16[2,6,32,384]{3,2,1,0:T(8,128)(2,1)}, u32[]{:S(2)}, u32[]{:S(2)}) collective-permute-start(bf16[2,6,32,384]{3,2,1,0:T(8,128)(2,1)} %get-tuple-element.37), channel_id=1, source_target_pairs={{8,24},{24,40},{40,56},{56,72},{72,88},{88,104},{104,120},{9,25},{... | collective-permute-start | bytes 884744 | tf_op jit(solution)/shard_map/ppermute | solution.py:543
  35.5 6.4 %collective-permute-start.4 = (bf16[2,6,32,384]{3,2,1,0:T(8,128)(2,1)}, bf16[2,6,32,384]{3,2,1,0:T(8,128)(2,1)}, u32[]{:S(2)}, u32[]{:S(2)}) collective-permute-start(bf16[2,6,32,384]{3,2,1,0:T(8,128)(2,1)} %get-tuple-element.37), channel_id=1, source_target_pairs={{8,16},{24,32},{40,48},{56,64},{72,80},{88,96},{104,112},{9,17},{2... | collective-permute-start | bytes 884744 | tf_op jit(solution)/shard_map/ppermute | solution.py:542
  37.5 20.6 %collective-permute-start.6 = (bf16[2,6,32,384]{3,2,1,0:T(8,128)(2,1)}, bf16[2,6,32,384]{3,2,1,0:T(8,128)(2,1)}, u32[]{:S(2)}, u32[]{:S(2)}) collective-permute-start(bf16[2,6,32,384]{3,2,1,0:T(8,128)(2,1)} %get-tuple-element.41), channel_id=1, source_target_pairs={{8,0},{16,8},{24,16},{32,24},{40,32},{48,40},{56,48},{64,56},{72,6... | collective-permute-start | bytes 884744 | tf_op jit(solution)/shard_map/ppermute | solution.py:505
  58.2 60.5 %all-to-all-start.1 = ((bf16[64,243,128]{2,1,0:T(8,128)(2,1)}), bf16[64,243,128]{2,1,0:T(8,128)(2,1)}, u32[]{:S(2)}, u32[]{:S(2)}) async-start(bf16[64,243,128]{2,1,0:T(8,128)(2,1)} %get-tuple-element.42), calls=%async_computation.1 | async-start | bytes 8126464 | tf_op jit(solution)/shard_map/all_to_all | solution.py:551
  86.7 26.3 %collective-permute-start.9 = (f32[16,32]{1,0:T(8,128)}, f32[16,32]{1,0:T(8,128)}, u32[]{:S(2)}, u32[]{:S(2)}) collective-permute-start(f32[16,32]{1,0:T(8,128)} %reduce_sum.18), channel_id=1, source_target_pairs={{0,3},{1,0},{2,1},{3,2},{4,7},{5,4},{6,5},{7,6},{8,11},{9,8},{10,9... | collective-permute-start | bytes 6152 | tf_op jit(solution)/shard_map/ppermute | solution.py:558
  88.9 24.4 %collective-permute-start.8 = (f32[16,32]{1,0:T(8,128)}, f32[16,32]{1,0:T(8,128)}, u32[]{:S(2)}, u32[]{:S(2)}) collective-permute-start(f32[16,32]{1,0:T(8,128)} %reduce_sum.18), channel_id=1, source_target_pairs={{0,2},{1,3},{2,0},{3,1},{4,6},{5,7},{6,4},{7,5},{8,10},{9,11},{10,... | collective-permute-start | bytes 6152 | tf_op jit(solution)/shard_map/ppermute | solution.py:558
  89.5 23.9 %collective-permute-start.7 = (f32[16,32]{1,0:T(8,128)}, f32[16,32]{1,0:T(8,128)}, u32[]{:S(2)}, u32[]{:S(2)}) collective-permute-start(f32[16,32]{1,0:T(8,128)} %reduce_sum.18), channel_id=1, source_target_pairs={{0,1},{1,2},{2,3},{3,0},{4,5},{5,6},{6,7},{7,4},{8,9},{9,10},{10,1... | collective-permute-start | bytes 6152 | tf_op jit(solution)/shard_map/ppermute | solution.py:558
  114.1 4.6 %collective-permute-start.10 = (f32[16,32]{1,0:T(8,128)S(1)}, f32[16,32]{1,0:T(8,128)S(1)}, u32[]{:S(2)}, u32[]{:S(2)}) collective-permute-start(f32[16,32]{1,0:T(8,128)S(1)} %add_add_fusion), channel_id=1, source_target_pairs={{0,4},{4,0},{1,5},{5,1},{2,6},{6,2},{3,7},{7,3},{8,12},{12,8},{9,1... | collective-permute-start | bytes 6152 | tf_op jit(solution)/shard_map/ppermute | solution.py:564
  118.7 8.3 %copy-start.1 = (bf16[8,4,32,384]{3,2,1,0:T(8,128)(2,1)S(1)}, bf16[8,4,32,384]{3,2,1,0:T(8,128)(2,1)}, u32[]{:S(2)}) copy-start(bf16[8,4,32,384]{3,2,1,0:T(8,128)(2,1)} %cot_ref.7) | copy-start | bytes 2359300
  118.7 8.3 %copy-start.2 = (f32[1024,384]{1,0:T(8,128)S(1)}, f32[1024,384]{1,0:T(8,128)}, u32[]{:S(2)}) copy-start(f32[1024,384]{1,0:T(8,128)} %get-tuple-element.51) | copy-start | bytes 4718596
  121.6 5.4 %copy-start = (bf16[8,4,32,384]{3,2,1,0:T(8,128)(2,1)S(1)}, bf16[8,4,32,384]{3,2,1,0:T(8,128)(2,1)}, u32[]{:S(2)}) copy-start(bf16[8,4,32,384]{3,2,1,0:T(8,128)(2,1)} %act_ref.3) | copy-start | bytes 2359300
  122.5 6.9 %collective-permute-start.11 = (f32[81,192]{1,0:T(8,128)S(1)}, f32[81,192]{1,0:T(8,128)}, u32[]{:S(2)}, u32[]{:S(2)}) collective-permute-start(f32[81,192]{1,0:T(8,128)S(1)} %fusion), channel_id=1, source_target_pairs={{0,8},{8,0},{1,9},{9,1},{2,10},{10,2},{3,11},{11,3},{4,12},{12,4},... | collective-permute-start | bytes 186632 | tf_op jit(solution)/shard_map/ppermute | solution.py:509

commit v2 on v1

--- a/solution.py
+++ b/solution.py
@@ -566,6 +566,7 @@
     total = jnp.sum(arrived.astype(f32), axis=0)
     sums = sums + other
     averages = per_channel(sums / CELL_COUNT)[:, None, None, :]
+    averages = lax.optimization_barrier(averages)
     first_avg, second_avg = averages[:SLOTS], averages[SLOTS:]
     wide_inv = inv[:, None, None, :]
     centred = (activations.astype(f32) - mean[:, None, None, :]) * wide_inv

time: 132 us -> 132 us (level)
  transfers between devices with their start and end apart: 14 -> 14, of which waited for: 5 -> 5; matrix products, arithmetic and copies ran while one was open for 9% -> 10% of each run, Pallas kernels for 39% -> 39%
where the time goes in v2:
time: 132 us
  Pallas kernels  55.3 us (42%)
  starting transfers between devices  44.4 us (34%)
  other arithmetic  12.9 us (10%)
  waiting for transfers between devices  12.4 us (9%)
  local copies, waits for them, and re-layouts  5.89 us (4%)
    pallas_call x1, Pallas kernels, backward_conv(): pl.pallas_call(backward_kernel, out_shape=(jax.ShapeDtypeStruct((POS, CHA...  17 us
    pallas_call x1, Pallas kernels, weight_terms(): pl.pallas_call(weight_kernel, out_shape=(jax.ShapeDtypeStruct((CHIPS, 3 *...  16.2 us
    pallas_call x1, Pallas kernels, forward_conv(): pl.pallas_call(forward_kernel, out_shape=jax.ShapeDtypeStruct((POS, CHAN)...  15.7 us
    all_to_all x1, starting transfers between devices, on_device(): arrived = lax.all_to_all(terms, CHIP_AXES, 0, 0)  9.83 us
    all_to_all x1, starting transfers between devices, on_device(): peers = lax.all_to_all(sums, ROW_AXES, 0, 0)  7.94 us
    ppermute x3, waiting for transfers between devices, on_device(): lax.ppermute(sums, 'x', [(i, (i + k) % 4) for i in range(4)])  7.6 us
    ppermute x3, starting transfers between devices, shift(): return lax.ppermute(values, axes, pairs)  7.15 us
    ppermute x3, starting transfers between devices, swap_cores(): return lax.ppermute(values, 'core', [(0, 1), (1, 0)])  6.87 us
  transfers between devices with their start and end apart: 14, of which 5 were waited for; matrix products, arithmetic and copies ran while one was open for 10% of the time, Pallas kernels for 39%

profile of v2, /device:TPU:1, one launch (start us, length us, event | category | flops | bytes accessed | tf_op | source)
XLA Modules:
  0.0 131.7 jit_solution(9910837988594268198)
XLA Ops:
  0.6 1.5 %collective-permute-start.2 = (bf16[8,4,32,384]{3,2,1,0:T(8,128)(2,1)}, bf16[8,4,32,384]{3,2,1,0:T(8,128)(2,1)}, u32[]{:S(2)}, u32[]{:S(2)}) collective-permute-start(bf16[8,4,32,384]{3,2,1,0:T(8,128)(2,1)} %cot_ref.7), channel_id=1, source_target_pairs={{0,8},{8,0},{1,9},{9,1},{2,10},{10,2},{3,11},{11,3},{4,12},{12,4},... | collective-permute-start | bytes 2359304 | tf_op jit(solution)/shard_map/ppermute | solution.py:509
  2.1 2.5 %local_sums.1 = (f32[8,16,384]{2,1,0:T(8,128)}, bf16[16,1,32,384]{3,2,1,0:T(8,128)(2,1)}, bf16[16,1,32,384]{3,2,1,0:T(8,128)(2,1)}) custom-call(bf16[8,4,32,384]{3,2,1,0:T(8,128)(2,1)} %act_ref.3, bf16[8,4,32,384]{3,2,1,0:T(8,128)(2,1)} %cot_ref.7), custom_call_target="tpu_custom_call" | custom-call | flops 1572864 | bytes 3145728 | tf_op jit(solution)/shard_map/local_sums/pallas_call | solution.py:416
  4.6 4.0 %collective-permute-start = (bf16[16,1,32,384]{3,2,1,0:T(8,128)(2,1)}, bf16[16,1,32,384]{3,2,1,0:T(8,128)(2,1)}, u32[]{:S(2)}, u32[]{:S(2)}) collective-permute-start(bf16[16,1,32,384]{3,2,1,0:T(8,128)(2,1)} %get-tuple-element.30), channel_id=1, source_target_pairs={{0,1},{1,2},{2,3},{3,4},{4,5},{5,6},{6,7},{8,9},{9,10},{10,11},{11... | collective-permute-start | bytes 1179656 | tf_op jit(solution)/shard_map/ppermute | solution.py:505
  8.6 1.3 collective-permute-start.1
  9.8 7.9 %all-to-all-start = ((f32[8,16,384]{2,1,0:T(8,128)}), f32[8,16,384]{2,1,0:T(8,128)}, u32[]{:S(2)}, u32[]{:S(2)}) async-start(f32[8,16,384]{2,1,0:T(8,128)} %get-tuple-element.32), calls=%async_computation | async-start | bytes 393216 | tf_op jit(solution)/shard_map/all_to_all | solution.py:527
  17.8 1.3 broadcast_in_dim.24.gain_ref
  19.1 1.3 broadcast_in_dim.25.bias_ref
  20.3 1.3 %fusion.4 = (s32[1]{0:T(128)}, s32[1]{0:T(128)}) fusion(s32[16]{0:T(128)} %param.8, s32[]{:T(128)S(6)} %select_n.30, s32[]{:T(128)S(6)} %select_n.31), kind=kLoop, calls=%fused_computation.19 | loop fusion | bytes 24 | tf_op jit(solution)/shard_map/dynamic_slice | solution.py:534
  21.7 1.9 %pad_add_fusion.place_ref = s32[4]{0:T(128)} fusion(s32[1]{0:T(128)} %get-tuple-element.66, s32[1]{0:T(128)} %bitcast.1, s32[1]{0:T(128)} %bitcast, s32[1]{0:T(128)} %get-tuple-element.65), kind=kLoop, calls=%fused_computation.15 | loop fusion | flops 12 | bytes 32 | tf_op jit(solution)/shard_map/stack | solution.py:535
  23.5 1.9 %all-to-all-done.peers_ref = f32[8,16,384]{2,1,0:T(8,128)} async-done(((f32[8,16,384]{2,1,0:T(8,128)}), f32[8,16,384]{2,1,0:T(8,128)}, u32[]{:S(2)}, u32[]{:S(2)}) %all-to-all-start) | async-done | bytes 196640 | tf_op jit(solution)/shard_map/all_to_all | solution.py:527
  25.5 0.0 collective-permute-done.low_ref.cot_low_ref
  25.5 0.0 collective-permute-done.1.high_ref.cot_high_ref
  25.5 0.0 collective-permute-done.2.other_cot_ref
  25.5 4.0 %make_hidden.1 = (bf16[8,6,32,384]{3,2,1,0:T(8,128)(2,1)}, bf16[2,6,32,384]{3,2,1,0:T(8,128)(2,1)}, bf16[2,6,32,384]{3,2,1,0:T(8,128)(2,1)}, f32[8,384]{1,0:T(8,128)}, f32[8,384]{1,0:T(8,128)}) custom-call(s32[4]{0:T(128)} %pad_add_fusion.place_ref, f32[8,16,384]{2,1,0:T(8,128)} %all-to-all-done.peers_ref, f32[384,384]{1,0:T(8,128)} %constant.41.clone.same_ref, ...), custom_call_target="tpu_custom_call" | custom-call | flops 15728640 | bytes 5242880 | tf_op jit(solution)/shard_map/make_hidden/pallas_call | solution.py:442
  29.4 1.8 %collective-permute-start.3 = (bf16[8,6,32,384]{3,2,1,0:T(8,128)(2,1)}, bf16[8,6,32,384]{3,2,1,0:T(8,128)(2,1)}, u32[]{:S(2)}, u32[]{:S(2)}) collective-permute-start(bf16[8,6,32,384]{3,2,1,0:T(8,128)(2,1)} %get-tuple-element.36.hidden_ref), channel_id=1, source_target_pairs={{0,8},{8,0},{1,9},{9,1},{2,10},{10,2},{3,11},{11,3},{4,12},{12,4},... | collective-permute-start | bytes 3538952 | tf_op jit(solution)/shard_map/ppermute | solution.py:509
  31.2 4.3 %collective-permute-start.5 = (bf16[2,6,32,384]{3,2,1,0:T(8,128)(2,1)}, bf16[2,6,32,384]{3,2,1,0:T(8,128)(2,1)}, u32[]{:S(2)}, u32[]{:S(2)}) collective-permute-start(bf16[2,6,32,384]{3,2,1,0:T(8,128)(2,1)} %get-tuple-element.37), channel_id=1, source_target_pairs={{8,24},{24,40},{40,56},{56,72},{72,88},{88,104},{104,120},{9,25},{... | collective-permute-start | bytes 884744 | tf_op jit(solution)/shard_map/ppermute | solution.py:543
  35.5 2.0 %collective-permute-start.4 = (bf16[2,6,32,384]{3,2,1,0:T(8,128)(2,1)}, bf16[2,6,32,384]{3,2,1,0:T(8,128)(2,1)}, u32[]{:S(2)}, u32[]{:S(2)}) collective-permute-start(bf16[2,6,32,384]{3,2,1,0:T(8,128)(2,1)} %get-tuple-element.37), channel_id=1, source_target_pairs={{8,16},{24,32},{40,48},{56,64},{72,80},{88,96},{104,112},{9,17},{2... | collective-permute-start | bytes 884744 | tf_op jit(solution)/shard_map/ppermute | solution.py:542
  37.5 1.9 %collective-permute-start.6 = (bf16[2,6,32,384]{3,2,1,0:T(8,128)(2,1)}, bf16[2,6,32,384]{3,2,1,0:T(8,128)(2,1)}, u32[]{:S(2)}, u32[]{:S(2)}) collective-permute-start(bf16[2,6,32,384]{3,2,1,0:T(8,128)(2,1)} %get-tuple-element.41), channel_id=1, source_target_pairs={{8,0},{16,8},{24,16},{32,24},{40,32},{48,40},{56,48},{64,56},{72,6... | collective-permute-start | bytes 884744 | tf_op jit(solution)/shard_map/ppermute | solution.py:505
  39.4 0.0 collective-permute-done.5.odd_ref
  39.4 2.5 %collective-permute-done.4.even_ref = bf16[2,6,32,384]{3,2,1,0:T(8,128)(2,1)} collective-permute-done((bf16[2,6,32,384]{3,2,1,0:T(8,128)(2,1)}, bf16[2,6,32,384]{3,2,1,0:T(8,128)(2,1)}, u32[]{:S(2)}, u32[]{:S(2)}) %collective-permute-start.4) | collective-permute-done | bytes 294944 | tf_op jit(solution)/shard_map/ppermute | solution.py:542
  41.9 0.0 collective-permute-done.3.other_ref
  41.9 16.2 %weight_terms.1 = (bf16[64,243,128]{2,1,0:T(8,128)(2,1)}, bf16[2,6,32,384]{3,2,1,0:T(8,128)(2,1)}) custom-call(s32[4]{0:T(128)} %pad_add_fusion.place_ref, bf16[8,6,32,384]{3,2,1,0:T(8,128)(2,1)} %get-tuple-element.36.hidden_ref, bf16[8,6,32,384]{3,2,1,0:T(8,128)(2,1)} %collective-permute-done.3.other_ref, ...), custom_call_target="tpu_custom_call" | custom-call | flops 8153726976 | bytes 12582912 | tf_op jit(solution)/shard_map/weight_terms/pallas_call | solution.py:481
  58.1 0.0 collective-permute-done.6.head_ref
  58.1 9.8 %all-to-all-start.1 = ((bf16[64,243,128]{2,1,0:T(8,128)(2,1)}), bf16[64,243,128]{2,1,0:T(8,128)(2,1)}, u32[]{:S(2)}, u32[]{:S(2)}) async-start(bf16[64,243,128]{2,1,0:T(8,128)(2,1)} %get-tuple-element.42), calls=%async_computation.1 | async-start | bytes 8126464 | tf_op jit(solution)/shard_map/all_to_all | solution.py:551
  68.0 17.0 %backward_conv.1 = (f32[1024,384]{1,0:T(8,128)}, f32[8,384]{1,0:T(8,128)}, f32[8,384]{1,0:T(8,128)}) custom-call(s32[4]{0:T(128)} %pad_add_fusion.place_ref, bf16[8,4,32,384]{3,2,1,0:T(8,128)(2,1)} %cot_ref.7, bf16[16,1,32,384]{3,2,1,0:T(8,128)(2,1)} %collective-permute-done.low_ref.cot_low_ref, ...), custom_call_target="tpu_custom_call" | custom-call | flops 8153726976 | bytes 12582912 | tf_op jit(solution)/shard_map/backward_conv/pallas_call | solution.py:391
  85.0 0.7 pad_maximum_fusion.3
  85.7 0.3 reshape.25
  86.0 0.7 reduce_sum.18
  86.7 2.2 %collective-permute-start.9 = (f32[16,32]{1,0:T(8,128)}, f32[16,32]{1,0:T(8,128)}, u32[]{:S(2)}, u32[]{:S(2)}) collective-permute-start(f32[16,32]{1,0:T(8,128)} %reduce_sum.18), channel_id=1, source_target_pairs={{0,3},{1,0},{2,1},{3,2},{4,7},{5,4},{6,5},{7,6},{8,11},{9,8},{10,9... | collective-permute-start | bytes 6152 | tf_op jit(solution)/shard_map/ppermute | solution.py:558
  88.9 0.6 collective-permute-start.8
  89.5 0.6 collective-permute-start.7
  90.0 15.7 %forward_conv.1 = bf16[1024,384]{1,0:T(8,128)(2,1)} custom-call(s32[4]{0:T(128)} %pad_add_fusion.place_ref, bf16[2,6,32,384]{3,2,1,0:T(8,128)(2,1)} %get-tuple-element.39.before_ref, bf16[8,6,32,384]{3,2,1,0:T(8,128)(2,1)} %get-tuple-element.36.hidden_ref, bf16[10368,384]{1,0:T(8,128)(2,1)} %w_ref.3, bf16[1024,384]{1,0:T(8,128)(2,1)} %bitcast.11), custom_call_target="tpu_custom_call" | custom-call | flops 8153726976 | bytes 12582912 | tf_op jit(solution)/shard_map/forward_conv/pallas_call | solution.py:367
  105.7 7.3 %collective-permute-done.9 = f32[16,32]{1,0:T(8,128)} collective-permute-done((f32[16,32]{1,0:T(8,128)}, f32[16,32]{1,0:T(8,128)}, u32[]{:S(2)}, u32[]{:S(2)}) %collective-permute-start.9) | collective-permute-done | bytes 2080 | tf_op jit(solution)/shard_map/ppermute | solution.py:558
  113.0 0.3 collective-permute-done.8
  113.3 0.0 collective-permute-done.7
  113.3 0.8 add_add_fusion
  114.1 3.0 %collective-permute-start.10 = (f32[16,32]{1,0:T(8,128)S(1)}, f32[16,32]{1,0:T(8,128)S(1)}, u32[]{:S(2)}, u32[]{:S(2)}) collective-permute-start(f32[16,32]{1,0:T(8,128)S(1)} %add_add_fusion), channel_id=1, source_target_pairs={{0,4},{4,0},{1,5},{5,1},{2,6},{6,2},{3,7},{7,3},{8,12},{12,8},{9,1... | collective-permute-start | bytes 6152 | tf_op jit(solution)/shard_map/ppermute | solution.py:564
  117.1 1.2 iota_compare_fusion
  118.2 0.0 copy-start.5
  118.2 0.4 collective-permute-done.10
  118.7 0.0 all-to-all-done.1
  118.7 0.0 copy-start.1
  118.7 0.0 copy-start.2
  118.7 2.9 %convert_reduce_fusion = f32[243,128]{1,0:T(8,128)S(1)} fusion(bf16[64,243,128]{2,1,0:T(8,128)(2,1)} %all-to-all-done.1), kind=kLoop, calls=%fused_computation | loop fusion | flops 3950208 | bytes 4105728 | tf_op jit(solution)/shard_map/reduce_sum | solution.py:566
  121.5 0.0 copy-start
  121.6 0.1 fusion.3
  121.7 0.0 copy-start.3
  121.7 0.7 fusion
  122.3 0.0 copy-done.3
  122.3 3.5 %collective-permute-start.11 = (f32[81,192]{1,0:T(8,128)}, f32[81,192]{1,0:T(8,128)}, u32[]{:S(2)}, u32[]{:S(2)}) collective-permute-start(f32[81,192]{1,0:T(8,128)} %fusion), channel_id=1, source_target_pairs={{0,8},{8,0},{1,9},{9,1},{2,10},{10,2},{3,11},{11,3},{4,12},{12,4},... | collective-permute-start | bytes 186632 | tf_op jit(solution)/shard_map/ppermute | solution.py:509
  125.9 0.1 broadcast_in_dim.27
  126.0 0.8 broadcast_in_dim_reshape.3
  126.8 0.7 slice_bitcast_fusion.1
  127.5 0.0 copy-done.5
  127.5 0.0 copy-done.1
  127.5 0.0 copy-done.2
  127.5 0.0 copy-done
  127.6 0.0 copy-start.4
  127.6 2.4 %add_select_fusion = f32[8,4,32,384]{3,2,1,0:T(8,128)} fusion(bf16[8,4,32,384]{3,2,1,0:T(8,128)(2,1)S(1)} %copy-done, f32[8,4,32,384]{3,2,1,0:T(8,128)S(1)} %bitcast.12, bf16[8,4,32,384]{3,2,1,0:T(8,128)(2,1)S(1)} %copy-done.1, f32[8,384]{1,0:T(8,128)S(1)} %get-tuple-element.64, f32[8,384]{1,0:T(8,128)S(1)} %copy-done.5, f32[8,384]{1,0:T(8,128)S(1)} %get-tuple-element.63, ...), kind=kLoop, calls=%fused_computation.1 | loop fusion | flops 3932160 | bytes 4767752 | tf_op jit(solution)/shard_map/jit(_where)/select_n | solution.py:577
  130.0 0.0 collective-permute-done.11
  130.0 0.0 copy-done.4
  130.0 0.9 broadcast_select_fusion.1
  130.9 0.8 pad_maximum_fusion
  (5 shorter events, 0.0 us)
Async XLA Ops:
  0.6 24.8 %collective-permute-start.2 = (bf16[8,4,32,384]{3,2,1,0:T(8,128)(2,1)}, bf16[8,4,32,384]{3,2,1,0:T(8,128)(2,1)}, u32[]{:S(2)}, u32[]{:S(2)}) collective-permute-start(bf16[8,4,32,384]{3,2,1,0:T(8,128)(2,1)} %cot_ref.7), channel_id=1, source_target_pairs={{0,8},{8,0},{1,9},{9,1},{2,10},{10,2},{3,11},{11,3},{4,12},{12,4},... | collective-permute-start | bytes 2359304 | tf_op jit(solution)/shard_map/ppermute | solution.py:509
  4.6 20.9 %collective-permute-start = (bf16[16,1,32,384]{3,2,1,0:T(8,128)(2,1)}, bf16[16,1,32,384]{3,2,1,0:T(8,128)(2,1)}, u32[]{:S(2)}, u32[]{:S(2)}) collective-permute-start(bf16[16,1,32,384]{3,2,1,0:T(8,128)(2,1)} %get-tuple-element.30), channel_id=1, source_target_pairs={{0,1},{1,2},{2,3},{3,4},{4,5},{5,6},{6,7},{8,9},{9,10},{10,11},{11... | collective-permute-start | bytes 1179656 | tf_op jit(solution)/shard_map/ppermute | solution.py:505
  8.6 16.9 %collective-permute-start.1 = (bf16[16,1,32,384]{3,2,1,0:T(8,128)(2,1)}, bf16[16,1,32,384]{3,2,1,0:T(8,128)(2,1)}, u32[]{:S(2)}, u32[]{:S(2)}) collective-permute-start(bf16[16,1,32,384]{3,2,1,0:T(8,128)(2,1)} %get-tuple-element.31), channel_id=1, source_target_pairs={{1,0},{2,1},{3,2},{4,3},{5,4},{6,5},{7,6},{9,8},{10,9},{11,10},{12... | collective-permute-start | bytes 1179656 | tf_op jit(solution)/shard_map/ppermute | solution.py:505
  9.8 15.6 %all-to-all-start = ((f32[8,16,384]{2,1,0:T(8,128)}), f32[8,16,384]{2,1,0:T(8,128)}, u32[]{:S(2)}, u32[]{:S(2)}) async-start(f32[8,16,384]{2,1,0:T(8,128)} %get-tuple-element.32), calls=%async_computation | async-start | bytes 393216 | tf_op jit(solution)/shard_map/all_to_all | solution.py:527
  29.4 12.5 %collective-permute-start.3 = (bf16[8,6,32,384]{3,2,1,0:T(8,128)(2,1)}, bf16[8,6,32,384]{3,2,1,0:T(8,128)(2,1)}, u32[]{:S(2)}, u32[]{:S(2)}) collective-permute-start(bf16[8,6,32,384]{3,2,1,0:T(8,128)(2,1)} %get-tuple-element.36.hidden_ref), channel_id=1, source_target_pairs={{0,8},{8,0},{1,9},{9,1},{2,10},{10,2},{3,11},{11,3},{4,12},{12,4},... | collective-permute-start | bytes 3538952 | tf_op jit(solution)/shard_map/ppermute | solution.py:509
  31.2 8.2 %collective-permute-start.5 = (bf16[2,6,32,384]{3,2,1,0:T(8,128)(2,1)}, bf16[2,6,32,384]{3,2,1,0:T(8,128)(2,1)}, u32[]{:S(2)}, u32[]{:S(2)}) collective-permute-start(bf16[2,6,32,384]{3,2,1,0:T(8,128)(2,1)} %get-tuple-element.37), channel_id=1, source_target_pairs={{8,24},{24,40},{40,56},{56,72},{72,88},{88,104},{104,120},{9,25},{... | collective-permute-start | bytes 884744 | tf_op jit(solution)/shard_map/ppermute | solution.py:543
  35.5 6.4 %collective-permute-start.4 = (bf16[2,6,32,384]{3,2,1,0:T(8,128)(2,1)}, bf16[2,6,32,384]{3,2,1,0:T(8,128)(2,1)}, u32[]{:S(2)}, u32[]{:S(2)}) collective-permute-start(bf16[2,6,32,384]{3,2,1,0:T(8,128)(2,1)} %get-tuple-element.37), channel_id=1, source_target_pairs={{8,16},{24,32},{40,48},{56,64},{72,80},{88,96},{104,112},{9,17},{2... | collective-permute-start | bytes 884744 | tf_op jit(solution)/shard_map/ppermute | solution.py:542
  37.5 20.6 %collective-permute-start.6 = (bf16[2,6,32,384]{3,2,1,0:T(8,128)(2,1)}, bf16[2,6,32,384]{3,2,1,0:T(8,128)(2,1)}, u32[]{:S(2)}, u32[]{:S(2)}) collective-permute-start(bf16[2,6,32,384]{3,2,1,0:T(8,128)(2,1)} %get-tuple-element.41), channel_id=1, source_target_pairs={{8,0},{16,8},{24,16},{32,24},{40,32},{48,40},{56,48},{64,56},{72,6... | collective-permute-start | bytes 884744 | tf_op jit(solution)/shard_map/ppermute | solution.py:505
  58.1 60.5 %all-to-all-start.1 = ((bf16[64,243,128]{2,1,0:T(8,128)(2,1)}), bf16[64,243,128]{2,1,0:T(8,128)(2,1)}, u32[]{:S(2)}, u32[]{:S(2)}) async-start(bf16[64,243,128]{2,1,0:T(8,128)(2,1)} %get-tuple-element.42), calls=%async_computation.1 | async-start | bytes 8126464 | tf_op jit(solution)/shard_map/all_to_all | solution.py:551
  86.7 26.3 %collective-permute-start.9 = (f32[16,32]{1,0:T(8,128)}, f32[16,32]{1,0:T(8,128)}, u32[]{:S(2)}, u32[]{:S(2)}) collective-permute-start(f32[16,32]{1,0:T(8,128)} %reduce_sum.18), channel_id=1, source_target_pairs={{0,3},{1,0},{2,1},{3,2},{4,7},{5,4},{6,5},{7,6},{8,11},{9,8},{10,9... | collective-permute-start | bytes 6152 | tf_op jit(solution)/shard_map/ppermute | solution.py:558
  88.9 24.4 %collective-permute-start.8 = (f32[16,32]{1,0:T(8,128)}, f32[16,32]{1,0:T(8,128)}, u32[]{:S(2)}, u32[]{:S(2)}) collective-permute-start(f32[16,32]{1,0:T(8,128)} %reduce_sum.18), channel_id=1, source_target_pairs={{0,2},{1,3},{2,0},{3,1},{4,6},{5,7},{6,4},{7,5},{8,10},{9,11},{10,... | collective-permute-start | bytes 6152 | tf_op jit(solution)/shard_map/ppermute | solution.py:558
  89.5 23.9 %collective-permute-start.7 = (f32[16,32]{1,0:T(8,128)}, f32[16,32]{1,0:T(8,128)}, u32[]{:S(2)}, u32[]{:S(2)}) collective-permute-start(f32[16,32]{1,0:T(8,128)} %reduce_sum.18), channel_id=1, source_target_pairs={{0,1},{1,2},{2,3},{3,0},{4,5},{5,6},{6,7},{7,4},{8,9},{9,10},{10,1... | collective-permute-start | bytes 6152 | tf_op jit(solution)/shard_map/ppermute | solution.py:558
  114.1 4.6 %collective-permute-start.10 = (f32[16,32]{1,0:T(8,128)S(1)}, f32[16,32]{1,0:T(8,128)S(1)}, u32[]{:S(2)}, u32[]{:S(2)}) collective-permute-start(f32[16,32]{1,0:T(8,128)S(1)} %add_add_fusion), channel_id=1, source_target_pairs={{0,4},{4,0},{1,5},{5,1},{2,6},{6,2},{3,7},{7,3},{8,12},{12,8},{9,1... | collective-permute-start | bytes 6152 | tf_op jit(solution)/shard_map/ppermute | solution.py:564
  118.2 9.3 %copy-start.5 = (f32[8,384]{1,0:T(8,128)S(1)}, f32[8,384]{1,0:T(8,128)}, u32[]{:S(2)}) copy-start(f32[8,384]{1,0:T(8,128)} %get-tuple-element.46.mean_ref) | copy-start | bytes 36868
  118.7 8.9 %copy-start.1 = (bf16[8,4,32,384]{3,2,1,0:T(8,128)(2,1)S(1)}, bf16[8,4,32,384]{3,2,1,0:T(8,128)(2,1)}, u32[]{:S(2)}) copy-start(bf16[8,4,32,384]{3,2,1,0:T(8,128)(2,1)} %cot_ref.7) | copy-start | bytes 2359300
  118.7 8.9 %copy-start.2 = (f32[1024,384]{1,0:T(8,128)S(1)}, f32[1024,384]{1,0:T(8,128)}, u32[]{:S(2)}) copy-start(f32[1024,384]{1,0:T(8,128)} %get-tuple-element.51) | copy-start | bytes 4718596
  121.5 6.0 %copy-start = (bf16[8,4,32,384]{3,2,1,0:T(8,128)(2,1)S(1)}, bf16[8,4,32,384]{3,2,1,0:T(8,128)(2,1)}, u32[]{:S(2)}) copy-start(bf16[8,4,32,384]{3,2,1,0:T(8,128)(2,1)} %act_ref.3) | copy-start | bytes 2359300
  121.7 0.7 copy-start.3
  122.3 7.6 %collective-permute-start.11 = (f32[81,192]{1,0:T(8,128)}, f32[81,192]{1,0:T(8,128)}, u32[]{:S(2)}, u32[]{:S(2)}) collective-permute-start(f32[81,192]{1,0:T(8,128)} %fusion), channel_id=1, source_target_pairs={{0,8},{8,0},{1,9},{9,1},{2,10},{10,2},{3,11},{11,3},{4,12},{12,4},... | collective-permute-start | bytes 186632 | tf_op jit(solution)/shard_map/ppermute | solution.py:509
  127.6 2.4 %copy-start.4 = (f32[81,128]{1,0:T(8,128)S(1)}, f32[81,128]{1,0:T(8,128)}, u32[]{:S(2)}) copy-start(f32[81,128]{1,0:T(8,128)} %copy-done.3) | copy-start | bytes 124420

commit v3 on v1

--- a/solution.py
+++ b/solution.py
@@ -20,7 +20,8 @@
 POS = SLOTS * CELLS
 WIDE = 3 * CHAN
 PIECE = 81
-CHIPS = 64
+DEVICES = 128
+SENT = PIECE + (PIECE + 1) // 2
 LANES = 128
 WIDE_CELLS = (ROWS + 2) * COLS
 CELL_COUNT = 8 * CELLS * (CHAN // GROUPS)
@@ -28,7 +29,6 @@
 
 TM = ("ylo", "z", "core")
 ROW_AXES = ("yhi", "x")
-CHIP_AXES = ("ylo", "z", "yhi", "x")
 ALL_AXES = TM + ROW_AXES
 
 bf16 = jnp.bfloat16
@@ -160,7 +160,7 @@
             second_ref[frame : frame + 1] = jnp.sum(pre_grad * centred, axis=0, keepdims=True)
 
 
-READY = ((0, 2), (2, 5), (5, 8))
+READY = ((0, 42), (42, 85), (85, 128))
 
 
 def weight_kernel(
@@ -237,7 +237,8 @@
 
     lax.fori_loop(0, SLOTS, move, 0, unroll=True)
 
-    upper = lax.broadcasted_iota(jnp.int32, (PIECE, LANES), 1) >= LANES // 2
+    short = SENT - PIECE
+    upper = lax.broadcasted_iota(jnp.int32, (short, LANES), 1) >= LANES // 2
     copies = []
     for a in range(3):
         window = jnp.concatenate(
@@ -255,19 +256,14 @@
                 sums[at : at + CHAN] = product[
                     b * CHAN : (b + 1) * CHAN, c * TILE : (c + 1) * TILE
                 ]
-        for chip in range(8 * READY[a][0], 8 * READY[a][1]):
-            start = 1296 * (chip // 8) + PIECE * (chip % 8)
-            first, second = sums[start : start + PIECE], sums[start + 648 : start + 648 + PIECE]
+        for device in range(*READY[a]):
+            piece = sums[device * PIECE : (device + 1) * PIECE]
+            inner = piece[:, LANES:]
             block = jnp.concatenate(
-                [
-                    first[:, :LANES],
-                    second[:, :LANES],
-                    jnp.where(upper, second[:, LANES:], first[:, LANES:]),
-                ],
-                axis=0,
+                [piece[:, :LANES], jnp.where(upper, inner[PIECE - short :], inner[:short])], axis=0
             )
-            packed[chip] = block.astype(bf16)
-        chips = pl.ds(8 * READY[a][0], 8 * (READY[a][1] - READY[a][0]))
+            packed[device] = block.astype(bf16)
+        chips = pl.ds(READY[a][0], READY[a][1] - READY[a][0])
         copies.append(pltpu.make_async_copy(packed.at[chips], out_ref.at[chips], sems.at[a]))
         copies[-1].start()
     for copy in copies:
@@ -481,7 +477,7 @@
     return pl.pallas_call(
         weight_kernel,
         out_shape=(
-            jax.ShapeDtypeStruct((CHIPS, 3 * PIECE, LANES), bf16),
+            jax.ShapeDtypeStruct((DEVICES, SENT, LANES), bf16),
             jax.ShapeDtypeStruct(pair, bf16),
         ),
         in_specs=[SMEM_SPEC] + [in_vmem] * 6,
@@ -491,7 +487,7 @@
             pltpu.VMEM((WIDE, 2 * (SLOTS + 2) * CELLS), bf16),
             pltpu.VMEM((2 * POS, 3 * TILE), bf16),
             pltpu.VMEM((9 * WIDE, TILE), f32),
-            pltpu.VMEM((CHIPS, 3 * PIECE, LANES), bf16),
+            pltpu.VMEM((DEVICES, SENT, LANES), bf16),
             pltpu.SemaphoreType.DMA((3,)),
         ],
         compiler_params=VMEM_LIMIT,
@@ -548,7 +544,7 @@
         place, wide_hidden, other_hidden, even, odd, cotangent, other_cot
     )
     terms, head = lax.optimization_barrier((terms, head))
-    arrived = lax.all_to_all(terms, CHIP_AXES, 0, 0)
+    arrived = lax.all_to_all(terms, ALL_AXES, 0, 0)
 
     low, high, _ = lax.optimization_barrier((low, high, terms))
     pre_grad, first_grad, second_grad = backward_conv(
@@ -563,7 +559,8 @@
     sums = sums + parts[0] + parts[1] + parts[2]
     other = lax.ppermute(sums, "yhi", [(0, 1), (1, 0)])
     other, arrived = lax.optimization_barrier((other, arrived))
-    total = jnp.sum(arrived.astype(f32), axis=0)
+    by_core = arrived.reshape(8, 2, 8, SENT, LANES)
+    total = jnp.sum(by_core.astype(f32), axis=(0, 2))
     sums = sums + other
     averages = per_channel(sums / CELL_COUNT)[:, None, None, :]
     first_avg, second_avg = averages[:SLOTS], averages[SLOTS:]
@@ -578,18 +575,11 @@
     frame_total = 1 + 4 * ((16 - 1) * 3 // 2)
     grad_scale = 1.0 / math.sqrt(frame_total * 8 * ROWS * COLS)
     total = total * grad_scale
-    shared = total[2 * PIECE :]
-    parts = [
-        jnp.concatenate(
-            [total[k * PIECE : (k + 1) * PIECE], shared[:, k * 64 : (k + 1) * 64]], axis=1
-        )
-        for k in range(2)
-    ]
-    mine = jnp.where(core == 0, parts[0], parts[1])
-    theirs = swap_cores(jnp.where(core == 0, parts[1], parts[0]))
-    first = jnp.where(core == 0, mine, theirs)
-    second = jnp.where(core == 0, theirs, mine)
-    weight_grad = jnp.concatenate([first, second[:, LANES:], second[:, :LANES]], axis=1)
+    outer = total[:, :PIECE]
+    inner = jnp.concatenate(
+        [total[:, PIECE:, : LANES // 2], total[:, PIECE + 1 :, LANES // 2 :]], axis=1
+    )
+    weight_grad = jnp.concatenate([outer[0], inner[0], inner[1], outer[1]], axis=1)
     return block_out, input_grad, weight_grad
 
 

time: 132 us -> 129 us (0.977)
  starting transfers between devices: 44.4 us -> 41.5 us
  waiting for transfers between devices: 13.1 us -> 14.9 us
  other arithmetic: 11.7 us -> 10.3 us
    ppermute x3 -> x2, starting transfers between devices: 6.96 us -> 3.32 us  [swap_cores(): return lax.ppermute(values, 'core', [(0, 1), (1, 0)])]
    ppermute x3, waiting for transfers between devices: 7.61 us -> 9.59 us  [on_device(): lax.ppermute(sums, 'x', [(i, (i + k) % 4) for i in range(4)])]
  transfers between devices with their start and end apart: 14 -> 13, of which waited for: 5 -> 5; matrix products, arithmetic and copies ran while one was open for 9% -> 7% of each run, Pallas kernels for 39% -> 40%
where the time goes in v3:
time: 129 us; the launch traced here: 128 us
  Pallas kernels  55.5 us (43%)
  starting transfers between devices  41.5 us (32%)
  waiting for transfers between devices  14.9 us (12%)
  other arithmetic  10.3 us (8%)
  local copies, waits for them, and re-layouts  4.73 us (4%)
    pallas_call x1, Pallas kernels, backward_conv(): pl.pallas_call(backward_kernel, out_shape=(jax.ShapeDtypeStruct((POS, CHA...  17 us
    pallas_call x1, Pallas kernels, weight_terms(): pl.pallas_call(weight_kernel, out_shape=(jax.ShapeDtypeStruct((DEVICES, S...  16.4 us
    pallas_call x1, Pallas kernels, forward_conv(): pl.pallas_call(forward_kernel, out_shape=jax.ShapeDtypeStruct((POS, CHAN)...  15.7 us
    all_to_all x1, starting transfers between devices, on_device(): arrived = lax.all_to_all(terms, ALL_AXES, 0, 0)  10.3 us
    ppermute x3, waiting for transfers between devices, on_device(): lax.ppermute(sums, 'x', [(i, (i + k) % 4) for i in range(4)])  9.59 us
    all_to_all x1, starting transfers between devices, on_device(): peers = lax.all_to_all(sums, ROW_AXES, 0, 0)  7.95 us
    ppermute x3, starting transfers between devices, shift(): return lax.ppermute(values, axes, pairs)  7.15 us
    ppermute x1, starting transfers between devices, on_device(): odd = lax.ppermute(last_pair, TM, [(i, i + 2) for i in range(1, 15, 2)])  4.27 us
  transfers between devices with their start and end apart: 13, of which 5 were waited for; matrix products, arithmetic and copies ran while one was open for 7% of the time, Pallas kernels for 40%

profile of v3, /device:TPU:1, one launch (start us, length us, event | category | flops | bytes accessed | tf_op | source)
XLA Modules:
  0.0 127.7 jit_solution(2887973910470543454)
XLA Ops:
  0.6 1.5 %collective-permute-start.2 = (bf16[8,4,32,384]{3,2,1,0:T(8,128)(2,1)}, bf16[8,4,32,384]{3,2,1,0:T(8,128)(2,1)}, u32[]{:S(2)}, u32[]{:S(2)}) collective-permute-start(bf16[8,4,32,384]{3,2,1,0:T(8,128)(2,1)} %cot_ref.7), channel_id=1, source_target_pairs={{0,8},{8,0},{1,9},{9,1},{2,10},{10,2},{3,11},{11,3},{4,12},{12,4},... | collective-permute-start | bytes 2359304 | tf_op jit(solution)/shard_map/ppermute | solution.py:505
  2.1 2.5 %local_sums.1 = (f32[8,16,384]{2,1,0:T(8,128)}, bf16[16,1,32,384]{3,2,1,0:T(8,128)(2,1)}, bf16[16,1,32,384]{3,2,1,0:T(8,128)(2,1)}) custom-call(bf16[8,4,32,384]{3,2,1,0:T(8,128)(2,1)} %act_ref.3, bf16[8,4,32,384]{3,2,1,0:T(8,128)(2,1)} %cot_ref.7), custom_call_target="tpu_custom_call" | custom-call | flops 1572864 | bytes 3145728 | tf_op jit(solution)/shard_map/local_sums/pallas_call | solution.py:412
  4.6 4.0 %collective-permute-start = (bf16[16,1,32,384]{3,2,1,0:T(8,128)(2,1)}, bf16[16,1,32,384]{3,2,1,0:T(8,128)(2,1)}, u32[]{:S(2)}, u32[]{:S(2)}) collective-permute-start(bf16[16,1,32,384]{3,2,1,0:T(8,128)(2,1)} %get-tuple-element.30), channel_id=1, source_target_pairs={{0,1},{1,2},{2,3},{3,4},{4,5},{5,6},{6,7},{8,9},{9,10},{10,11},{11... | collective-permute-start | bytes 1179656 | tf_op jit(solution)/shard_map/ppermute | solution.py:501
  8.6 1.3 %collective-permute-start.1 = (bf16[16,1,32,384]{3,2,1,0:T(8,128)(2,1)}, bf16[16,1,32,384]{3,2,1,0:T(8,128)(2,1)}, u32[]{:S(2)}, u32[]{:S(2)}) collective-permute-start(bf16[16,1,32,384]{3,2,1,0:T(8,128)(2,1)} %get-tuple-element.31), channel_id=1, source_target_pairs={{1,0},{2,1},{3,2},{4,3},{5,4},{6,5},{7,6},{9,8},{10,9},{11,10},{12... | collective-permute-start | bytes 1179656 | tf_op jit(solution)/shard_map/ppermute | solution.py:501
  9.9 7.9 %all-to-all-start = ((f32[8,16,384]{2,1,0:T(8,128)}), f32[8,16,384]{2,1,0:T(8,128)}, u32[]{:S(2)}, u32[]{:S(2)}) async-start(f32[8,16,384]{2,1,0:T(8,128)} %get-tuple-element.32), calls=%async_computation | async-start | bytes 393216 | tf_op jit(solution)/shard_map/all_to_all | solution.py:523
  17.8 1.3 broadcast_in_dim.26.gain_ref
  19.1 1.3 broadcast_in_dim.27.bias_ref
  20.4 1.4 %fusion.4 = (s32[1]{0:T(128)}, s32[1]{0:T(128)}) fusion(s32[16]{0:T(128)} %param.8, s32[]{:T(128)S(6)} %select_n.10, s32[]{:T(128)S(6)} %select_n.11), kind=kLoop, calls=%fused_computation.18 | loop fusion | bytes 24 | tf_op jit(solution)/shard_map/dynamic_slice | solution.py:530
  21.7 2.0 %pad_add_fusion.place_ref = s32[4]{0:T(128)} fusion(s32[1]{0:T(128)} %get-tuple-element.64, s32[1]{0:T(128)} %bitcast.1, s32[1]{0:T(128)} %bitcast, s32[1]{0:T(128)} %get-tuple-element.63), kind=kLoop, calls=%fused_computation.15 | loop fusion | flops 12 | bytes 32 | tf_op jit(solution)/shard_map/stack | solution.py:531
  23.7 1.8 %all-to-all-done.peers_ref = f32[8,16,384]{2,1,0:T(8,128)} async-done(((f32[8,16,384]{2,1,0:T(8,128)}), f32[8,16,384]{2,1,0:T(8,128)}, u32[]{:S(2)}, u32[]{:S(2)}) %all-to-all-start) | async-done | bytes 196640 | tf_op jit(solution)/shard_map/all_to_all | solution.py:523
  25.5 0.0 collective-permute-done.low_ref.cot_low_ref
  25.5 0.0 collective-permute-done.1.high_ref.cot_high_ref
  25.5 0.0 collective-permute-done.2.other_cot_ref
  25.5 4.0 %make_hidden.1 = (bf16[8,6,32,384]{3,2,1,0:T(8,128)(2,1)}, bf16[2,6,32,384]{3,2,1,0:T(8,128)(2,1)}, bf16[2,6,32,384]{3,2,1,0:T(8,128)(2,1)}, f32[8,384]{1,0:T(8,128)}, f32[8,384]{1,0:T(8,128)}) custom-call(s32[4]{0:T(128)} %pad_add_fusion.place_ref, f32[8,16,384]{2,1,0:T(8,128)} %all-to-all-done.peers_ref, f32[384,384]{1,0:T(8,128)} %constant.41.clone.same_ref, ...), custom_call_target="tpu_custom_call" | custom-call | flops 15728640 | bytes 5242880 | tf_op jit(solution)/shard_map/make_hidden/pallas_call | solution.py:438
  29.4 1.8 %collective-permute-start.3 = (bf16[8,6,32,384]{3,2,1,0:T(8,128)(2,1)}, bf16[8,6,32,384]{3,2,1,0:T(8,128)(2,1)}, u32[]{:S(2)}, u32[]{:S(2)}) collective-permute-start(bf16[8,6,32,384]{3,2,1,0:T(8,128)(2,1)} %get-tuple-element.36.hidden_ref), channel_id=1, source_target_pairs={{0,8},{8,0},{1,9},{9,1},{2,10},{10,2},{3,11},{11,3},{4,12},{12,4},... | collective-permute-start | bytes 3538952 | tf_op jit(solution)/shard_map/ppermute | solution.py:505
  31.3 4.3 %collective-permute-start.5 = (bf16[2,6,32,384]{3,2,1,0:T(8,128)(2,1)}, bf16[2,6,32,384]{3,2,1,0:T(8,128)(2,1)}, u32[]{:S(2)}, u32[]{:S(2)}) collective-permute-start(bf16[2,6,32,384]{3,2,1,0:T(8,128)(2,1)} %get-tuple-element.37), channel_id=1, source_target_pairs={{8,24},{24,40},{40,56},{56,72},{72,88},{88,104},{104,120},{9,25},{... | collective-permute-start | bytes 884744 | tf_op jit(solution)/shard_map/ppermute | solution.py:539
  35.5 2.0 %collective-permute-start.4 = (bf16[2,6,32,384]{3,2,1,0:T(8,128)(2,1)}, bf16[2,6,32,384]{3,2,1,0:T(8,128)(2,1)}, u32[]{:S(2)}, u32[]{:S(2)}) collective-permute-start(bf16[2,6,32,384]{3,2,1,0:T(8,128)(2,1)} %get-tuple-element.37), channel_id=1, source_target_pairs={{8,16},{24,32},{40,48},{56,64},{72,80},{88,96},{104,112},{9,17},{2... | collective-permute-start | bytes 884744 | tf_op jit(solution)/shard_map/ppermute | solution.py:538
  37.5 1.9 %collective-permute-start.6 = (bf16[2,6,32,384]{3,2,1,0:T(8,128)(2,1)}, bf16[2,6,32,384]{3,2,1,0:T(8,128)(2,1)}, u32[]{:S(2)}, u32[]{:S(2)}) collective-permute-start(bf16[2,6,32,384]{3,2,1,0:T(8,128)(2,1)} %get-tuple-element.41), channel_id=1, source_target_pairs={{8,0},{16,8},{24,16},{32,24},{40,32},{48,40},{56,48},{64,56},{72,6... | collective-permute-start | bytes 884744 | tf_op jit(solution)/shard_map/ppermute | solution.py:501
  39.5 0.0 collective-permute-done.5.odd_ref
  39.5 2.5 %collective-permute-done.4.even_ref = bf16[2,6,32,384]{3,2,1,0:T(8,128)(2,1)} collective-permute-done((bf16[2,6,32,384]{3,2,1,0:T(8,128)(2,1)}, bf16[2,6,32,384]{3,2,1,0:T(8,128)(2,1)}, u32[]{:S(2)}, u32[]{:S(2)}) %collective-permute-start.4) | collective-permute-done | bytes 294944 | tf_op jit(solution)/shard_map/ppermute | solution.py:538
  41.9 0.0 collective-permute-done.3.other_ref
  41.9 16.4 %weight_terms.1 = (bf16[128,122,128]{2,1,0:T(8,128)(2,1)}, bf16[2,6,32,384]{3,2,1,0:T(8,128)(2,1)}) custom-call(s32[4]{0:T(128)} %pad_add_fusion.place_ref, bf16[8,6,32,384]{3,2,1,0:T(8,128)(2,1)} %get-tuple-element.36.hidden_ref, bf16[8,6,32,384]{3,2,1,0:T(8,128)(2,1)} %collective-permute-done.3.other_ref, ...), custom_call_target="tpu_custom_call" | custom-call | flops 8153726976 | bytes 12582912 | tf_op jit(solution)/shard_map/weight_terms/pallas_call | solution.py:477
  58.3 0.0 collective-permute-done.6.head_ref
  58.3 10.3 %all-to-all-start.1 = ((bf16[128,122,128]{2,1,0:T(8,128)(2,1)}), bf16[128,122,128]{2,1,0:T(8,128)(2,1)}, u32[]{:S(2)}, u32[]{:S(2)}) async-start(bf16[128,122,128]{2,1,0:T(8,128)(2,1)} %get-tuple-element.42), calls=%async_computation.1 | async-start | bytes 8388608 | tf_op jit(solution)/shard_map/all_to_all | solution.py:547
  68.7 17.0 %backward_conv.1 = (f32[1024,384]{1,0:T(8,128)}, f32[8,384]{1,0:T(8,128)}, f32[8,384]{1,0:T(8,128)}) custom-call(s32[4]{0:T(128)} %pad_add_fusion.place_ref, bf16[8,4,32,384]{3,2,1,0:T(8,128)(2,1)} %cot_ref.7, bf16[16,1,32,384]{3,2,1,0:T(8,128)(2,1)} %collective-permute-done.low_ref.cot_low_ref, ...), custom_call_target="tpu_custom_call" | custom-call | flops 8153726976 | bytes 12582912 | tf_op jit(solution)/shard_map/backward_conv/pallas_call | solution.py:387
  85.7 0.7 pad_maximum_fusion.2
  86.4 0.3 reshape.32
  86.7 0.7 reduce_sum.18
  87.4 2.6 %collective-permute-start.9 = (f32[16,32]{1,0:T(8,128)}, f32[16,32]{1,0:T(8,128)}, u32[]{:S(2)}, u32[]{:S(2)}) collective-permute-start(f32[16,32]{1,0:T(8,128)} %reduce_sum.18), channel_id=1, source_target_pairs={{0,3},{1,0},{2,1},{3,2},{4,7},{5,4},{6,5},{7,6},{8,11},{9,8},{10,9... | collective-permute-start | bytes 6152 | tf_op jit(solution)/shard_map/ppermute | solution.py:554
  90.0 0.6 collective-permute-start.8
  90.6 0.6 collective-permute-start.7
  91.2 15.7 %forward_conv.1 = bf16[1024,384]{1,0:T(8,128)(2,1)} custom-call(s32[4]{0:T(128)} %pad_add_fusion.place_ref, bf16[2,6,32,384]{3,2,1,0:T(8,128)(2,1)} %get-tuple-element.39.before_ref, bf16[8,6,32,384]{3,2,1,0:T(8,128)(2,1)} %get-tuple-element.36.hidden_ref, bf16[10368,384]{1,0:T(8,128)(2,1)} %w_ref.3, bf16[1024,384]{1,0:T(8,128)(2,1)} %bitcast.17), custom_call_target="tpu_custom_call" | custom-call | flops 8153726976 | bytes 12582912 | tf_op jit(solution)/shard_map/forward_conv/pallas_call | solution.py:363
  106.9 8.1 %collective-permute-done.9 = f32[16,32]{1,0:T(8,128)} collective-permute-done((f32[16,32]{1,0:T(8,128)}, f32[16,32]{1,0:T(8,128)}, u32[]{:S(2)}, u32[]{:S(2)}) %collective-permute-start.9) | collective-permute-done | bytes 2080 | tf_op jit(solution)/shard_map/ppermute | solution.py:554
  114.9 1.5 %collective-permute-done.8 = f32[16,32]{1,0:T(8,128)} collective-permute-done((f32[16,32]{1,0:T(8,128)}, f32[16,32]{1,0:T(8,128)}, u32[]{:S(2)}, u32[]{:S(2)}) %collective-permute-start.8) | collective-permute-done | bytes 2080 | tf_op jit(solution)/shard_map/ppermute | solution.py:554
  116.4 0.0 collective-permute-done.7
  116.4 0.8 add_add_fusion
  117.2 2.7 %collective-permute-start.10 = (f32[16,32]{1,0:T(8,128)S(1)}, f32[16,32]{1,0:T(8,128)S(1)}, u32[]{:S(2)}, u32[]{:S(2)}) collective-permute-start(f32[16,32]{1,0:T(8,128)S(1)} %add_add_fusion), channel_id=1, source_target_pairs={{0,4},{4,0},{1,5},{5,1},{2,6},{6,2},{3,7},{7,3},{8,12},{12,8},{9,1... | collective-permute-start | bytes 6152 | tf_op jit(solution)/shard_map/ppermute | solution.py:560
  119.9 0.7 iota_compare_fusion
  120.6 1.0 collective-permute-done.10
  121.6 0.0 all-to-all-done.1
  121.6 0.0 copy-start.2
  121.6 3.0 %convert_reduce_fusion = f32[2,122,128]{2,1,0:T(8,128)S(1)} fusion(bf16[8,2,8,122,128]{4,3,2,1,0:T(8,128)(2,1)} %bitcast.11), kind=kLoop, calls=%fused_computation | loop fusion | flops 3966464 | bytes 4122624 | tf_op jit(solution)/shard_map/reduce_sum | solution.py:563
  124.6 0.0 copy-start
  124.6 0.0 copy-start.1
  124.6 0.0 copy-start.3
  124.6 0.0 copy-start.4
  124.7 0.1 slice.43
  124.8 0.1 broadcast_in_dim.29
  124.9 0.1 sub.25
  125.0 0.1 broadcast_in_dim.30
  125.1 0.1 mul.48
  125.2 0.8 pad_maximum_fusion
  126.0 0.0 copy-done.2
  126.0 0.0 copy-done
  126.0 0.0 copy-done.1
  126.0 0.0 copy-done.3
  126.0 0.0 copy-done.4
  126.0 1.7 %add_select_fusion = f32[8,4,32,384]{3,2,1,0:T(8,128)} fusion(bf16[8,4,32,384]{3,2,1,0:T(8,128)(2,1)S(1)} %copy-done, f32[8,4,32,384]{3,2,1,0:T(8,128)S(1)} %bitcast.18, bf16[8,4,32,384]{3,2,1,0:T(8,128)(2,1)S(1)} %copy-done.1, f32[8,384]{1,0:T(8,128)S(1)} %mul.48, f32[8,384]{1,0:T(8,128)S(1)} %copy-done.3, f32[8,384]{1,0:T(8,128)S(1)} %sub.25, ...), kind=kLoop, calls=%fused_computation.1 | loop fusion | flops 3932160 | bytes 4767752 | tf_op jit(solution)/shard_map/jit(_where)/select_n | solution.py:573
  (6 shorter events, 0.1 us)
Async XLA Ops:
  0.6 24.8 %collective-permute-start.2 = (bf16[8,4,32,384]{3,2,1,0:T(8,128)(2,1)}, bf16[8,4,32,384]{3,2,1,0:T(8,128)(2,1)}, u32[]{:S(2)}, u32[]{:S(2)}) collective-permute-start(bf16[8,4,32,384]{3,2,1,0:T(8,128)(2,1)} %cot_ref.7), channel_id=1, source_target_pairs={{0,8},{8,0},{1,9},{9,1},{2,10},{10,2},{3,11},{11,3},{4,12},{12,4},... | collective-permute-start | bytes 2359304 | tf_op jit(solution)/shard_map/ppermute | solution.py:505
  4.6 20.9 %collective-permute-start = (bf16[16,1,32,384]{3,2,1,0:T(8,128)(2,1)}, bf16[16,1,32,384]{3,2,1,0:T(8,128)(2,1)}, u32[]{:S(2)}, u32[]{:S(2)}) collective-permute-start(bf16[16,1,32,384]{3,2,1,0:T(8,128)(2,1)} %get-tuple-element.30), channel_id=1, source_target_pairs={{0,1},{1,2},{2,3},{3,4},{4,5},{5,6},{6,7},{8,9},{9,10},{10,11},{11... | collective-permute-start | bytes 1179656 | tf_op jit(solution)/shard_map/ppermute | solution.py:501
  8.6 16.9 %collective-permute-start.1 = (bf16[16,1,32,384]{3,2,1,0:T(8,128)(2,1)}, bf16[16,1,32,384]{3,2,1,0:T(8,128)(2,1)}, u32[]{:S(2)}, u32[]{:S(2)}) collective-permute-start(bf16[16,1,32,384]{3,2,1,0:T(8,128)(2,1)} %get-tuple-element.31), channel_id=1, source_target_pairs={{1,0},{2,1},{3,2},{4,3},{5,4},{6,5},{7,6},{9,8},{10,9},{11,10},{12... | collective-permute-start | bytes 1179656 | tf_op jit(solution)/shard_map/ppermute | solution.py:501
  9.9 15.6 %all-to-all-start = ((f32[8,16,384]{2,1,0:T(8,128)}), f32[8,16,384]{2,1,0:T(8,128)}, u32[]{:S(2)}, u32[]{:S(2)}) async-start(f32[8,16,384]{2,1,0:T(8,128)} %get-tuple-element.32), calls=%async_computation | async-start | bytes 393216 | tf_op jit(solution)/shard_map/all_to_all | solution.py:523
  29.4 12.5 %collective-permute-start.3 = (bf16[8,6,32,384]{3,2,1,0:T(8,128)(2,1)}, bf16[8,6,32,384]{3,2,1,0:T(8,128)(2,1)}, u32[]{:S(2)}, u32[]{:S(2)}) collective-permute-start(bf16[8,6,32,384]{3,2,1,0:T(8,128)(2,1)} %get-tuple-element.36.hidden_ref), channel_id=1, source_target_pairs={{0,8},{8,0},{1,9},{9,1},{2,10},{10,2},{3,11},{11,3},{4,12},{12,4},... | collective-permute-start | bytes 3538952 | tf_op jit(solution)/shard_map/ppermute | solution.py:505
  31.3 8.2 %collective-permute-start.5 = (bf16[2,6,32,384]{3,2,1,0:T(8,128)(2,1)}, bf16[2,6,32,384]{3,2,1,0:T(8,128)(2,1)}, u32[]{:S(2)}, u32[]{:S(2)}) collective-permute-start(bf16[2,6,32,384]{3,2,1,0:T(8,128)(2,1)} %get-tuple-element.37), channel_id=1, source_target_pairs={{8,24},{24,40},{40,56},{56,72},{72,88},{88,104},{104,120},{9,25},{... | collective-permute-start | bytes 884744 | tf_op jit(solution)/shard_map/ppermute | solution.py:539
  35.5 6.4 %collective-permute-start.4 = (bf16[2,6,32,384]{3,2,1,0:T(8,128)(2,1)}, bf16[2,6,32,384]{3,2,1,0:T(8,128)(2,1)}, u32[]{:S(2)}, u32[]{:S(2)}) collective-permute-start(bf16[2,6,32,384]{3,2,1,0:T(8,128)(2,1)} %get-tuple-element.37), channel_id=1, source_target_pairs={{8,16},{24,32},{40,48},{56,64},{72,80},{88,96},{104,112},{9,17},{2... | collective-permute-start | bytes 884744 | tf_op jit(solution)/shard_map/ppermute | solution.py:538
  37.5 20.8 %collective-permute-start.6 = (bf16[2,6,32,384]{3,2,1,0:T(8,128)(2,1)}, bf16[2,6,32,384]{3,2,1,0:T(8,128)(2,1)}, u32[]{:S(2)}, u32[]{:S(2)}) collective-permute-start(bf16[2,6,32,384]{3,2,1,0:T(8,128)(2,1)} %get-tuple-element.41), channel_id=1, source_target_pairs={{8,0},{16,8},{24,16},{32,24},{40,32},{48,40},{56,48},{64,56},{72,6... | collective-permute-start | bytes 884744 | tf_op jit(solution)/shard_map/ppermute | solution.py:501
  58.3 63.3 %all-to-all-start.1 = ((bf16[128,122,128]{2,1,0:T(8,128)(2,1)}), bf16[128,122,128]{2,1,0:T(8,128)(2,1)}, u32[]{:S(2)}, u32[]{:S(2)}) async-start(bf16[128,122,128]{2,1,0:T(8,128)(2,1)} %get-tuple-element.42), calls=%async_computation.1 | async-start | bytes 8388608 | tf_op jit(solution)/shard_map/all_to_all | solution.py:547
  87.4 27.5 %collective-permute-start.9 = (f32[16,32]{1,0:T(8,128)}, f32[16,32]{1,0:T(8,128)}, u32[]{:S(2)}, u32[]{:S(2)}) collective-permute-start(f32[16,32]{1,0:T(8,128)} %reduce_sum.18), channel_id=1, source_target_pairs={{0,3},{1,0},{2,1},{3,2},{4,7},{5,4},{6,5},{7,6},{8,11},{9,8},{10,9... | collective-permute-start | bytes 6152 | tf_op jit(solution)/shard_map/ppermute | solution.py:554
  90.0 26.4 %collective-permute-start.8 = (f32[16,32]{1,0:T(8,128)}, f32[16,32]{1,0:T(8,128)}, u32[]{:S(2)}, u32[]{:S(2)}) collective-permute-start(f32[16,32]{1,0:T(8,128)} %reduce_sum.18), channel_id=1, source_target_pairs={{0,2},{1,3},{2,0},{3,1},{4,6},{5,7},{6,4},{7,5},{8,10},{9,11},{10,... | collective-permute-start | bytes 6152 | tf_op jit(solution)/shard_map/ppermute | solution.py:554
  90.6 25.8 %collective-permute-start.7 = (f32[16,32]{1,0:T(8,128)}, f32[16,32]{1,0:T(8,128)}, u32[]{:S(2)}, u32[]{:S(2)}) collective-permute-start(f32[16,32]{1,0:T(8,128)} %reduce_sum.18), channel_id=1, source_target_pairs={{0,1},{1,2},{2,3},{3,0},{4,5},{5,6},{6,7},{7,4},{8,9},{9,10},{10,1... | collective-permute-start | bytes 6152 | tf_op jit(solution)/shard_map/ppermute | solution.py:554
  117.2 4.4 %collective-permute-start.10 = (f32[16,32]{1,0:T(8,128)S(1)}, f32[16,32]{1,0:T(8,128)S(1)}, u32[]{:S(2)}, u32[]{:S(2)}) collective-permute-start(f32[16,32]{1,0:T(8,128)S(1)} %add_add_fusion), channel_id=1, source_target_pairs={{0,4},{4,0},{1,5},{5,1},{2,6},{6,2},{3,7},{7,3},{8,12},{12,8},{9,1... | collective-permute-start | bytes 6152 | tf_op jit(solution)/shard_map/ppermute | solution.py:560
  121.6 4.4 %copy-start.2 = (f32[1024,384]{1,0:T(8,128)S(1)}, f32[1024,384]{1,0:T(8,128)}, u32[]{:S(2)}) copy-start(f32[1024,384]{1,0:T(8,128)} %get-tuple-element.51) | copy-start | bytes 4718596
  124.6 1.4 %copy-start = (bf16[8,4,32,384]{3,2,1,0:T(8,128)(2,1)S(1)}, bf16[8,4,32,384]{3,2,1,0:T(8,128)(2,1)}, u32[]{:S(2)}) copy-start(bf16[8,4,32,384]{3,2,1,0:T(8,128)(2,1)} %act_ref.3) | copy-start | bytes 2359300
  124.6 1.4 %copy-start.1 = (bf16[8,4,32,384]{3,2,1,0:T(8,128)(2,1)S(1)}, bf16[8,4,32,384]{3,2,1,0:T(8,128)(2,1)}, u32[]{:S(2)}) copy-start(bf16[8,4,32,384]{3,2,1,0:T(8,128)(2,1)} %cot_ref.7) | copy-start | bytes 2359300
  124.6 1.4 %copy-start.3 = (f32[8,384]{1,0:T(8,128)S(1)}, f32[8,384]{1,0:T(8,128)}, u32[]{:S(2)}) copy-start(f32[8,384]{1,0:T(8,128)} %get-tuple-element.46.mean_ref) | copy-start | bytes 36868
  124.6 1.4 %copy-start.4 = (f32[8,384]{1,0:T(8,128)S(1)}, f32[8,384]{1,0:T(8,128)}, u32[]{:S(2)}) copy-start(f32[8,384]{1,0:T(8,128)} %get-tuple-element.47.inv_ref) | copy-start | bytes 36868
